TPU v7x, 128 devices: a whole 4x4x4 slice. The times are simulated.
128 devices in a mesh: tm: 2 (over core), layer: 2 (over x_lo), mode: 32 (over z, y, x_hi).
Axes of the slice: x: 4 (x_hi: 2, x_lo: 2; x = x_hi * 2 + x_lo), y: 4, z: 4, core: 2. Of those that a mesh axis runs over, the one named last changes fastest.
Arguments:
- innovation: bfloat16 [2, 2, 32, 2048, 2048], P(None, 'layer', 'tm', 'mode'), may hold values from -6 to 6
- retention: float32 [2, 2048, 2048], P('layer', 'mode'), may hold values from 0.8 to 0.999
- rytov_filter: float32 [2, 2048, 2048], P('layer', 'mode'), may hold values from 0.1 to 1
- wind_shift: float32 [2, 32, 2], P('layer', 'tm'), may hold values from -3 to 3
- start_state: float32 [2, 2, 2048, 2048], P(None, 'layer', 'mode'), may hold values from -8 to 8
Outputs:
- log_amplitude: float32 [32, 2048, 2048], P(('tm', 'layer'), 'mode')
All inputs are finite; a program needn't handle non-finite values.
Results may differ from a plain program's by a relative error of at most 0.014.
Values may be sent and summed in bfloat16 or wider, within the bound.
No kernel may reach another device: no remote copies, remote signals or barrier semaphores. Data moves between devices by JAX's collectives and lax.ppermute only.
A program may use at most 128 MiB of HBM per device.

v0:
```python
import math

import jax
import jax.numpy as jnp
from jax import lax
from jax.sharding import PartitionSpec as P


def carried_in(value, axis, join, neutral):
    place = lax.axis_index(axis)
    gathered = jax.tree.map(
        lambda a, kind: lax.all_gather(a.astype(kind), axis),
        value,
        (jnp.bfloat16, jnp.bfloat16, jnp.bfloat16, jnp.bfloat16),
    )
    state = jax.tree.map(lambda a, e: jnp.zeros_like(a) + jnp.asarray(e, a.dtype), value, neutral)

    def one(step, state):
        return join(
            state,
            jax.tree.map(
                lambda a, own: lax.dynamic_index_in_dim(a, step, 0, False).astype(own.dtype),
                gathered,
                value,
            ),
        )

    return lax.fori_loop(0, place, one, state)


def shards(innovation, retention, rytov_filter, wind_shift, start_state):
    slab_rows = retention.shape[1]
    grid_size = retention.shape[2]
    angle_step = 2.0 * math.pi / grid_size
    retain_rate = retention[0]
    filter_gain = rytov_filter[0]
    row_ids = lax.axis_index("mode") * slab_rows + lax.iota(jnp.int32, slab_rows)
    col_ids = lax.iota(jnp.int32, grid_size)
    wave_x = jnp.where(row_ids >= grid_size // 2, row_ids - grid_size, row_ids).astype(jnp.float32)[
        :, None
    ]
    wave_y = jnp.where(col_ids >= grid_size // 2, col_ids - grid_size, col_ids).astype(jnp.float32)[
        None, :
    ]
    noise_real = innovation[0, 0]
    noise_imag = innovation[1, 0]
    wind_steps = wind_shift[0]

    def rotation(wind_step):
        phase_angle = (wave_x * wind_step[0] + wave_y * wind_step[1]) * angle_step
        return (retain_rate * jnp.cos(phase_angle), retain_rate * jnp.sin(phase_angle))

    def compose(running, inputs):
        prod_real, prod_imag, acc_real, acc_imag = running
        wind_step, fresh_real, fresh_imag = inputs
        gain_real, gain_imag = rotation(wind_step)
        return (
            (
                gain_real * prod_real - gain_imag * prod_imag,
                gain_real * prod_imag + gain_imag * prod_real,
                gain_real * acc_real - gain_imag * acc_imag + fresh_real.astype(jnp.float32),
                gain_real * acc_imag + gain_imag * acc_real + fresh_imag.astype(jnp.float32),
            ),
            None,
        )

    unit_real = jnp.ones((slab_rows, grid_size), jnp.float32)
    zero_field = jnp.zeros((slab_rows, grid_size), jnp.float32)
    local_map, unused = lax.scan(
        compose,
        (unit_real, zero_field, zero_field, zero_field),
        (wind_steps, noise_real, noise_imag),
    )
    prod_real, prod_imag, acc_real, acc_imag = local_map
    start_real = start_state[0, 0]
    start_imag = start_state[1, 0]

    def combine(earlier, later_map):
        return (
            later_map[0] * earlier[0] - later_map[1] * earlier[1],
            later_map[0] * earlier[1] + later_map[1] * earlier[0],
            later_map[0] * earlier[2] - later_map[1] * earlier[3] + later_map[2],
            later_map[0] * earlier[3] + later_map[1] * earlier[2] + later_map[3],
        )

    prefix = carried_in(
        (prod_real, prod_imag, acc_real, acc_imag),
        "tm",
        combine,
        (unit_real, zero_field, zero_field, zero_field),
    )
    enter_real = prefix[0] * start_real - prefix[1] * start_imag + prefix[2]
    enter_imag = prefix[0] * start_imag + prefix[1] * start_real + prefix[3]

    def advance(running, inputs):
        real_state, imag_state = running
        wind_step, fresh_real, fresh_imag = inputs
        gain_real, gain_imag = rotation(wind_step)
        next_real = gain_real * real_state - gain_imag * imag_state + fresh_real.astype(jnp.float32)
        next_imag = gain_real * imag_state + gain_imag * real_state + fresh_imag.astype(jnp.float32)
        filtered = jnp.concatenate(
            [filter_gain * next_real, filter_gain * next_imag], axis=0
        ).astype(jnp.bfloat16)
        return ((next_real, next_imag), filtered)

    final_state, layer_terms = lax.scan(
        advance, (enter_real, enter_imag), (wind_steps, noise_real, noise_imag)
    )
    wide_terms = layer_terms.astype(jnp.float32)
    summed = lax.psum_scatter(
        wide_terms.astype(jnp.bfloat16), "layer", scatter_dimension=0, tiled=True
    )
    product = col_ids[:, None] * col_ids[None, :] % grid_size
    phase_grid = product.astype(jnp.float32) * angle_step
    cos_low = jnp.cos(phase_grid).astype(jnp.bfloat16)
    sin_low = jnp.sin(phase_grid).astype(jnp.bfloat16)
    first_half = jnp.einsum("frk,ky->fyr", summed, cos_low, preferred_element_type=jnp.float32)
    second_half = jnp.einsum("frk,ky->fyr", summed, sin_low, preferred_element_type=jnp.float32)
    half_real = first_half[..., :slab_rows] - second_half[..., slab_rows:]
    half_imag = second_half[..., :slab_rows] + first_half[..., slab_rows:]
    columns = jnp.concatenate([half_real, half_imag], axis=-1).astype(jnp.bfloat16)[:, None]
    mode_parts = lax.axis_size("mode")
    inverse_table = jnp.concatenate(
        [
            cos_low.reshape(mode_parts, slab_rows, grid_size),
            -sin_low.reshape(mode_parts, slab_rows, grid_size),
        ],
        axis=1,
    )
    return jnp.einsum(
        "fmyr,mrx->fyx",
        lax.all_to_all(columns, "mode", split_axis=2, concat_axis=1, tiled=True),
        inverse_table,
        preferred_element_type=jnp.float32,
    ) * (1.0 / grid_size)


def solution(mesh):
    return jax.shard_map(
        shards,
        mesh=mesh,
        in_specs=(
            P(None, "layer", "tm", "mode", None),
            P("layer", "mode", None),
            P("layer", "mode", None),
            P("layer", "tm", None),
            P(None, "layer", "mode", None),
        ),
        out_specs=P(("tm", "layer"), "mode", None),
        check_vma=False,
    )
```

profile of v0, /device:TPU:1, one launch (start us, length us, event | category | flops | bytes accessed | tf_op | source)
XLA Modules:
  0.0 562.2 jit_solution(5013545429546333407)
XLA Ops:
  6.6 6.2 %slice_bitcast_fusion = (bf16[16,64,2048]{2,1,0:T(8,128)(2,1)}, bf16[16,64,2048]{2,1,0:T(8,128)(2,1)}) fusion(bf16[2,1,16,64,2048]{4,3,2,1,0:T(8,128)(2,1)} %param.11), kind=kLoop, calls=%fused_computation.90 | loop fusion | bytes 16777216 | tf_op jit(solution)/shard_map/squeeze | solution.py:46
  12.8 92.2 %while.50 = (s32[]{:T(128)}, f32[64,2048]{1,0:T(8,128)S(1)}, f32[64,2048]{1,0:T(8,128)S(1)}, f32[64,2048]{1,0:T(8,128)S(1)}, f32[64,2048]{1,0:T(8,128)S(1)}, /*i...) while((s32[]{:T(128)}, f32[64,2048]{1,0:T(8,128)S(1)}, ...), condition=%wide.region_1.2_spmd.clone, body=%wide.region_0.1_spmd.clone.sunk | while | flops 3156355 | bytes 5259955 | solution.py:69
  14.8 3.7 convert_add_fusion.7
  20.6 3.7 convert_add_fusion.7
  26.3 3.7 convert_add_fusion.7
  32.1 3.7 convert_add_fusion.7
  37.9 3.7 convert_add_fusion.7
  43.6 3.7 convert_add_fusion.7
  49.4 3.7 convert_add_fusion.7
  55.2 3.7 convert_add_fusion.7
  60.9 3.7 convert_add_fusion.7
  66.7 3.7 convert_add_fusion.7
  72.5 3.7 convert_add_fusion.7
  78.2 3.7 convert_add_fusion.7
  84.0 3.7 convert_add_fusion.7
  89.8 3.7 convert_add_fusion.7
  95.5 3.7 convert_add_fusion.7
  101.3 3.7 convert_add_fusion.7
  105.1 3.2 all-gather
  108.3 2.3 all-gather.1
  119.7 118.4 %while.49 = (s32[]{:T(128)}, f32[64,2048]{1,0:T(8,128)}, f32[64,2048]{1,0:T(8,128)S(1)}, bf16[16,128,2048]{2,1,0:T(8,128)(2,1)}, f32[16,2]{0,1:T(2,128)S(1)}, /*...) while((s32[]{:T(128)}, f32[64,2048]{1,0:T(8,128)}, ...), condition=%wide.region_5.6_spmd.clone, body=%wide.region_4.5_spmd.clone.sunk | while | flops 3418498 | bytes 5260449 | solution.py:106
  121.6 4.6 fusion.100
  129.0 4.6 fusion.100
  136.4 4.6 fusion.100
  143.8 4.6 fusion.100
  151.2 4.6 fusion.100
  158.6 4.6 fusion.100
  166.0 4.6 fusion.100
  173.4 4.6 fusion.100
  180.8 4.6 fusion.100
  188.2 4.6 fusion.100
  195.6 4.6 fusion.100
  203.0 4.6 fusion.100
  210.4 4.6 fusion.100
  217.8 4.6 fusion.100
  225.2 4.6 fusion.100
  232.6 4.6 fusion.100
  238.1 62.7 %fusion.84 = bf16[2048,2048,1]{1,0,2:T(8,128)(2,1)} fusion(), kind=kLoop, calls=%fused_computation.79.clone.clone.clone.clone.1 | loop fusion | flops 62914560 | bytes 8388608 | tf_op jit(solution)/shard_map/frk,ky->fyr/dot_general | solution.py:118
  300.8 62.2 %fusion.86 = bf16[2048,2048,1]{1,0,2:T(8,128)(2,1)} fusion(), kind=kLoop, calls=%fused_computation.77.clone.clone.clone.clone.1 | loop fusion | flops 62914560 | bytes 8388608 | tf_op jit(solution)/shard_map/frk,ky->fyr/dot_general | solution.py:117
  362.9 12.6 %fusion.50 = f32[8,2048,128]{1,2,0:T(8,128)S(1)} fusion(bf16[8,128,2048]{2,1,0:T(8,128)(2,1)} %reduce-scatter.2.cloned.1.call-done, bf16[2048,2048,1]{1,0,2:T(8,128)(2,1)} %fusion.84), kind=kOutput, calls=%fused_computation.82 | convolution fusion | flops 8589934592 | bytes 20971520 | tf_op jit(solution)/shard_map/frk,ky->fyr/dot_general | solution.py:118
  375.6 10.9 %fusion.53 = f32[8,2048,128]{1,2,0:T(8,128)S(1)} fusion(bf16[8,128,2048]{2,1,0:T(8,128)(2,1)} %reduce-scatter.2.cloned.1.call-done, bf16[2048,2048,1]{1,0,2:T(8,128)(2,1)S(1)} %copy-done.2), kind=kOutput, calls=%fused_computation.83 | convolution fusion | flops 8589934592 | bytes 20971520 | tf_op jit(solution)/shard_map/frk,ky->fyr/dot_general | solution.py:117
  387.9 2.6 pad_maximum_fusion
  390.5 6.8 %copy.8 = bf16[8,1,2048,128]{3,0,1,2:T(8,128)(2,1)} copy(bf16[8,1,2048,128]{2,3,0,1:T(8,128)(2,1)} %pad_maximum_fusion) | data formatting | bytes 8388608 | tf_op jit(solution)/shard_map/concatenate | solution.py:121
  397.2 11.0 %all-to-all-start = ((bf16[8,1,2048,128]{3,0,1,2:T(8,128)(2,1)}), bf16[8,1,2048,128]{3,0,1,2:T(8,128)(2,1)}, u32[]{:S(2)}, u32[]{:S(2)}) async-start(bf16[8,1,2048,128]{3,0,1,2:T(8,128)(2,1)} %copy.8), calls=%async_computation.1 | async-start | bytes 8388608 | tf_op jit(solution)/shard_map/all_to_all | solution.py:132
  408.2 64.4 %cosine_convert_fusion = bf16[32,64,2048]{2,1,0:T(8,128)(2,1)} fusion(s32[32,64]{1,0:T(8,128)S(1)} %multiply_add_fusion.1), kind=kLoop, calls=%fused_computation.68 | loop fusion | flops 62914560 | bytes 8396800 | tf_op jit(solution)/shard_map/convert_element_type | solution.py:115
  472.6 65.3 %fusion.47 = bf16[32,64,2048]{2,1,0:T(8,128)(2,1)} fusion(s32[32,64]{1,0:T(8,128)S(1)} %multiply_add_fusion.1), kind=kLoop, calls=%fused_computation.81 | loop fusion | flops 75497472 | bytes 8396800 | tf_op jit(solution)/shard_map/neg | solution.py:126
  538.0 2.9 copy.9
  542.6 12.7 %bitcast_multiply_fusion = f32[8,64,2048]{2,1,0:T(8,128)} fusion(bf16[8,32,64,128]{3,2,1,0:T(8,128)(2,1)S(1)} %bitcast.149, bf16[32,64,2048]{2,1,0:T(8,128)(2,1)} %fusion.47, bf16[32,64,2048]{2,1,0:T(8,128)(2,1)S(1)} %copy-done.1), kind=kOutput, calls=%fused_computation.89 | convolution fusion | flops 8624537600 | bytes 25165824 | tf_op jit(solution)/shard_map/fmyr,mrx->fyx/dot_general | solution.py:130
  (176 shorter events, 89.7 us)
Async XLA Ops:
  6.5 356.4 %reduce-scatter.2.cloned.1.call-start = ((), (), s32[]{:S(2)}) async-start(), calls=%async_computation.2 | async-start | bytes 12582912 | tf_op jit(solution)/shard_map/reduce_scatter | solution.py:110
  6.5 6.2 %copy-start = (f32[1,64,2048]{2,1,0:T(8,128)S(1)}, f32[1,64,2048]{2,1,0:T(8,128)}, u32[]{:S(2)}) copy-start(f32[1,64,2048]{2,1,0:T(8,128)} %param.12) | copy-start | bytes 1572868
  6.5 6.2 %copy-start.3 = (f32[1,16,2]{1,2,0:T(2,128)S(1)}, f32[1,16,2]{1,2,0:T(2,128)}, u32[]{:S(2)}) copy-start(f32[1,16,2]{1,2,0:T(2,128)} %param.14) | copy-start | bytes 388
  362.9 12.6 %copy-start.2 = (bf16[2048,2048,1]{1,0,2:T(8,128)(2,1)S(1)}, bf16[2048,2048,1]{1,0,2:T(8,128)(2,1)}, u32[]{:S(2)}) copy-start(bf16[2048,2048,1]{1,0,2:T(8,128)(2,1)} %fusion.86) | copy-start | bytes 25165828
  397.2 140.7 %all-to-all-start = ((bf16[8,1,2048,128]{3,0,1,2:T(8,128)(2,1)}), bf16[8,1,2048,128]{3,0,1,2:T(8,128)(2,1)}, u32[]{:S(2)}, u32[]{:S(2)}) async-start(bf16[8,1,2048,128]{3,0,1,2:T(8,128)(2,1)} %copy.8), calls=%async_computation.1 | async-start | bytes 8388608 | tf_op jit(solution)/shard_map/all_to_all | solution.py:132
  537.9 4.6 copy-start.1
Sparse Core Ops, SparseCore 0:
  238.2 103.6 reduce-scatter.1
where the time goes:
time: 566 us; the launch traced here: 562 us
  other arithmetic  451 us (80%)
  local copies, waits for them, and re-layouts  38.8 us (7%)
  matrix products  36.3 us (6%)
  between operations  13.5 us (2%)
  starting transfers between devices  11 us (2%)
  blocking collectives  10.2 us (2%)
    concatenate x16, other arithmetic, advance(): jnp.concatenate([filter_gain * next_real, filter_gain * next_imag], axis=0)  74.2 us
    neg x1, other arithmetic, shards(): -sin_low.reshape(mode_parts, slab_rows, grid_size)  65.3 us
    convert_element_type x1, other arithmetic, shards(): cos_low = jnp.cos(phase_grid).astype(jnp.bfloat16)  64.4 us
    dot_general x1, other arithmetic, shards(): jnp.einsum('frk,ky->fyr', summed, sin_low, preferred_element_type=jnp.flo...  62.7 us
    dot_general x1, other arithmetic, shards(): jnp.einsum('frk,ky->fyr', summed, cos_low, preferred_element_type=jnp.flo...  62.2 us
    add x16, other arithmetic, compose(): gain_real * acc_imag + gain_imag * acc_real + fresh_imag.astype(jnp.float32)  59.6 us
    mul x64, other arithmetic, rotation(): phase_angle = (wave_x * wind_step[0] + wave_y * wind_step[1]) * angle_step  41.4 us
    slice x32, local copies, waits for them, and re-layouts, rotation(): phase_angle = (wave_x * wind_step[0] + wave_y * wind_step[1]) * angle_step  18.7 us
  transfers between devices with their start and end apart: 2, of which 0 were waited for; matrix products, arithmetic and copies ran while one was open for 45% of the time, Pallas kernels for 0%

commit v1 on v0

v1 whole, which is shorter than its diff:
```python
import math

import jax
import jax.numpy as jnp
import numpy as np
from jax import lax
from jax.experimental import pallas as pl
from jax.experimental.pallas import tpu as pltpu
from jax.sharding import PartitionSpec as P

F32, BF16 = jnp.float32, jnp.bfloat16
ROWS = 16
VMEM = 56 * 1024 * 1024


def trig(n):
    k = np.arange(n, dtype=np.int64)
    prod = (k[:, None] * k[None, :]) % n
    ang = np.arange(n, dtype=np.float64) * (2.0 * math.pi / n)
    return np.cos(ang)[prod], np.sin(ang)[prod]


def tables(n, parts):
    cos, sin = trig(n)
    half, slab = n // 2, n // parts
    rows = np.concatenate([cos[:, :half], -sin[:, :half]], 1)
    first = rows.reshape(half, 2, n).transpose(1, 0, 2)
    second = np.stack(
        [cos.reshape(parts, slab, n), -sin.reshape(parts, slab, n)], 1
    ).reshape(2 * n, n) * (1.0 / n)
    bf = jnp.bfloat16
    return first.astype(bf), second.astype(bf)


def scan_kernel(flag, enter, noise, keep, filt, ea, eb, *rest):
    z, last = rest[-2:]
    steps = noise.shape[1]
    n = noise.shape[3]
    half = n // 2

    @pl.when(flag[0] == 1)
    def _():
        def lanes(j, carry):
            at = [pl.ds(pl.multiple_of(j * 128 + h * half, 128), 128) for h in range(2)]
            re = [enter[0, :, c].astype(F32) for c in at]
            im = [enter[1, :, c].astype(F32) for c in at]
            kp = [keep[:, c] for c in at]
            ft = [filt[:, c] for c in at]
            for t in range(steps):
                ar, ai = ea[0, t], ea[1, t]
                tr, ti = [], []
                for h in range(2):
                    br, bi = eb[0, t : t + 1, at[h]], eb[1, t : t + 1, at[h]]
                    gr = kp[h] * (ar * br - ai * bi)
                    gi = kp[h] * (ar * bi + ai * br)
                    nr = gr * re[h] - gi * im[h] + noise[0, t, :, at[h]].astype(F32)
                    ni = gr * im[h] + gi * re[h] + noise[1, t, :, at[h]].astype(F32)
                    re[h], im[h] = nr, ni
                    tr.append(ft[h] * nr)
                    ti.append(ft[h] * ni)
                for p in range(2):
                    pr = tr[0] + tr[1] if p == 0 else tr[0] - tr[1]
                    pi = ti[0] + ti[1] if p == 0 else ti[0] - ti[1]
                    z[p, t, 0, :, at[0]] = pr.astype(BF16)
                    z[p, t, 0, :, at[1]] = pi.astype(BF16)
                    z[p, t, 1, :, at[0]] = pi.astype(BF16)
                    z[p, t, 1, :, at[1]] = (-pr).astype(BF16)
            for h in range(2):
                last[0, :, at[h]] = re[h].astype(BF16)
                last[1, :, at[h]] = im[h].astype(BF16)
            return carry

        lax.fori_loop(0, half // 128, lanes, 0)


def scan_call(flag, enter, noise, keep, filt, ea, eb, z=None):
    steps, slab, n = noise.shape[1:]
    blocks = slab // ROWS

    def src(i, f):
        return jnp.where(f[0] == 1, i, 0)

    def dst(i, f):
        return jnp.where(f[0] == 1, i, blocks)

    in_specs = [
        pl.BlockSpec((2, ROWS, n), lambda i, f: (0, src(i, f), 0)),
        pl.BlockSpec((2, steps, ROWS, n), lambda i, f: (0, 0, src(i, f), 0)),
        pl.BlockSpec((ROWS, n), lambda i, f: (src(i, f), 0)),
        pl.BlockSpec((ROWS, n), lambda i, f: (src(i, f), 0)),
        pl.BlockSpec((2, steps, ROWS, 128), lambda i, f: (0, 0, src(i, f), 0)),
        pl.BlockSpec((2, steps, n), lambda i, f: (0, 0, 0)),
    ]
    args = [flag, enter, noise, keep, filt, ea, eb]
    alias = {}
    if z is not None:
        in_specs.append(pl.BlockSpec(memory_space=pl.ANY))
        args.append(z)
        alias = {7: 0}
    return pl.pallas_call(
        scan_kernel,
        out_shape=(
            jax.ShapeDtypeStruct((2, steps, 2, slab + ROWS, n), BF16),
            jax.ShapeDtypeStruct((2, slab + ROWS, n), BF16),
        ),
        grid_spec=pltpu.PrefetchScalarGridSpec(
            num_scalar_prefetch=1,
            grid=(blocks,),
            in_specs=in_specs,
            out_specs=[
                pl.BlockSpec((2, steps, 2, ROWS, n), lambda i, f: (0, 0, 0, dst(i, f), 0)),
                pl.BlockSpec((2, ROWS, n), lambda i, f: (0, dst(i, f), 0)),
            ],
        ),
        input_output_aliases=alias,
        compiler_params=pltpu.CompilerParams(vmem_limit_bytes=VMEM),
        name="scan",
    )(*args)


def first_kernel(table, z, out):
    owners, parts, frames = out.shape[:3]
    rows = out.shape[3] // 2
    for p in range(2):
        right = z[p].reshape(owners * frames * 128, z.shape[-1])
        acc = lax.dot_general(
            table[p], right, (((1,), (1,)), ((), ())), preferred_element_type=F32
        ).astype(BF16)
        for o in range(owners):
            for f in range(frames):
                c = (o * frames + f) * 128
                out[o, :, f, p * rows : (p + 1) * rows, :] = acc[:, c : c + 128].reshape(
                    parts, rows, 128
                )


def first_call(table, z, chunk, frames, parts, slab):
    n = z.shape[-1]
    group = 8
    return pl.pallas_call(
        first_kernel,
        out_shape=jax.ShapeDtypeStruct((2, parts, frames, slab, 128), BF16),
        grid=(parts // group,),
        in_specs=[
            pl.BlockSpec((2, group * slab // 2, n), lambda i: (0, i, 0)),
            pl.BlockSpec((2, 2, frames, 2, slab, n), lambda i: (0, 0, chunk, 0, 0, 0)),
        ],
        out_specs=pl.BlockSpec((2, group, frames, slab, 128), lambda i: (0, i, 0, 0, 0)),
        compiler_params=pltpu.CompilerParams(vmem_limit_bytes=VMEM),
        cost_estimate=pl.CostEstimate(
            flops=2 * n * n * 2 * frames * 128, bytes_accessed=24 << 20, transcendentals=0
        ),
        name="first",
    )(table, z)


def second_kernel(table, got, *rest):
    out, left, rows = rest[-3:]
    parts, frames, slab = got.shape[1:4]
    half = slab // 2

    @pl.when(pl.program_id(0) == 0)
    def _():
        for m in range(parts):
            both = got[0, m].astype(F32) + got[1, m].astype(F32)
            for f in range(frames):
                for p in range(2):
                    rows[m % 4, pl.ds(f * slab + p, half, stride=2), :] = both[
                        f, p * half : (p + 1) * half
                    ]
            left[:, m * 128 : (m + 1) * 128] = rows[m % 4].astype(BF16)

    acc = jnp.dot(left[...], table[...], preferred_element_type=F32)
    out[...] = acc.reshape(frames, slab, acc.shape[-1])


def second_call(table, got, chunk, total, out=None):
    parts, frames, slab = got.shape[1:4]
    depth, n = table.shape
    tile = 512
    in_specs = [
        pl.BlockSpec((depth, tile), lambda i: (0, i)),
        pl.BlockSpec((2, parts, frames, slab, 128), lambda i: (0, 0, 0, 0, 0)),
    ]
    args = [table, got]
    alias = {}
    if out is not None:
        in_specs.append(pl.BlockSpec(memory_space=pl.ANY))
        args.append(out)
        alias = {2: 0}
    return pl.pallas_call(
        second_kernel,
        out_shape=jax.ShapeDtypeStruct((total, slab, n), F32),
        grid=(n // tile,),
        in_specs=in_specs,
        out_specs=pl.BlockSpec((frames, slab, tile), lambda i: (chunk, 0, i)),
        scratch_shapes=[
            pltpu.VMEM((frames * slab, depth), BF16),
            pltpu.VMEM((4, frames * slab, 128), F32),
        ],
        input_output_aliases=alias,
        compiler_params=pltpu.CompilerParams(vmem_limit_bytes=VMEM),
        cost_estimate=pl.CostEstimate(
            flops=2 * depth * n * frames * slab, bytes_accessed=24 << 20, transcendentals=0
        ),
        name="second",
    )(*args)


CHUNKS = 2


def shards(innovation, retention, rytov_filter, wind_shift, start_state):
    noise = innovation[:, 0]
    keep, filt = retention[0], rytov_filter[0]
    wind = wind_shift[0]
    steps, slab, n = noise.shape[1:]
    parts = lax.axis_size("mode")
    total = steps // 2
    frames = total // CHUNKS
    first, second = tables(n, parts)

    def waves(k):
        return jnp.where(k >= n // 2, k - n, k).astype(F32)

    angle_step = 2.0 * math.pi / n
    rows = lax.axis_index("mode") * slab + lax.iota(jnp.int32, slab)
    pa = wind[:, 0:1] * (waves(rows) * angle_step)[None]
    pb = wind[:, 1:2] * (waves(lax.iota(jnp.int32, n)) * angle_step)[None]
    ea = jnp.broadcast_to(jnp.stack([jnp.cos(pa), jnp.sin(pa)])[..., None], (2, steps, slab, 128))
    eb = jnp.stack([jnp.cos(pb), jnp.sin(pb)])

    core = lax.axis_index("tm").astype(jnp.int32)
    z, last = scan_call((1 - core)[None], start_state[:, 0], noise, keep, filt, ea, eb)
    enter = lax.ppermute(last[:, :slab], "tm", [(0, 1)])
    z, _ = scan_call(core[None], enter, noise, keep, filt, ea, eb, z)
    z = z.reshape(2, 2, total, 2, slab + ROWS, n)

    out = None
    for c in range(CHUNKS):
        part = first_call(first, z, c, frames, parts, slab)
        got = lax.all_to_all(
            part.reshape(2 * parts, frames, slab, 128), ("layer", "mode"), 0, 0, tiled=True
        ).reshape(2, parts, frames, slab, 128)
        out = second_call(second, got, c, total, out)
    return out


def solution(mesh):
    return jax.shard_map(
        shards,
        mesh=mesh,
        in_specs=(
            P(None, "layer", "tm", "mode", None),
            P("layer", "mode", None),
            P("layer", "mode", None),
            P("layer", "tm", None),
            P(None, "layer", "mode", None),
        ),
        out_specs=P(("tm", "layer"), "mode", None),
        check_vma=False,
    )
```

time: 566 us -> 180 us (0.32)
  other arithmetic: 451 us -> 1.43 us
  waiting for transfers between devices: 0.02 us -> 80 us
  Pallas kernels: 0 us -> 71.4 us
  matrix products: 36.3 us -> 0 us
  local copies, waits for them, and re-layouts: 38.8 us -> 3.94 us
  between operations: 13.5 us -> 0.05 us
  starting transfers between devices: 11 us -> 21.6 us
  blocking collectives: 10.2 us -> 0 us
    dot_general x2 -> x0, other arithmetic: 125 us -> none  [the longest x1 62.7 us: shards(): jnp.einsum('frk,ky->fyr', summed, sin_low, preferred_element_type=jnp.flo...]
    concatenate x18 -> x0, other arithmetic: 78.1 us -> none  [the longest x16 74.2 us: advance(): jnp.concatenate([filter_gain * next_real, filter_gain * next_imag], axis=0)]
    pallas_call x0 -> x6, Pallas kernels: none -> 71.4 us  [the longest x2 29.2 us: first_call(): pl.pallas_call(first_kernel, out_shape=jax.ShapeDtypeStruct((2, parts, fr...]
    all_to_all x1 -> x2, waiting for transfers between devices: 0.01 us -> 66.6 us  [shards(): lax.all_to_all(part.reshape(2 * parts, frames, slab, 128), ('layer', 'mod...]
    neg x1 -> x0, other arithmetic: 65.3 us -> none  [shards(): -sin_low.reshape(mode_parts, slab_rows, grid_size)]
    convert_element_type x5 -> x0, other arithmetic: 64.5 us -> none  [the longest x1 64.4 us: shards(): cos_low = jnp.cos(phase_grid).astype(jnp.bfloat16)]
    add x18 -> x0, other arithmetic: 63.5 us -> none  [the longest x16 59.6 us: compose(): gain_real * acc_imag + gain_imag * acc_real + fresh_imag.astype(jnp.float32)]
    mul x65 -> x2, other arithmetic: 41.4 us -> 0.01 us  [the longest x1 0.01 us: shards(): pa = wind[:, 0:1] * (waves(rows) * angle_step)[None]]
  transfers between devices with their start and end apart: 2 -> 3, of which waited for: 0 -> 3; matrix products, arithmetic and copies ran while one was open for 45% -> 0% of each run, Pallas kernels for 0% -> 15%
where the time goes in v1:
time: 180 us; the launch traced here: 178 us
  waiting for transfers between devices  80 us (44%)
  Pallas kernels  71.4 us (40%)
  starting transfers between devices  21.6 us (12%)
  local copies, waits for them, and re-layouts  3.94 us (2%)
    all_to_all x2, waiting for transfers between devices, shards(): lax.all_to_all(part.reshape(2 * parts, frames, slab, 128), ('layer', 'mod...  66.6 us
    pallas_call x2, Pallas kernels, first_call(): pl.pallas_call(first_kernel, out_shape=jax.ShapeDtypeStruct((2, parts, fr...  29.2 us
    pallas_call x2, Pallas kernels, second_call(): pl.pallas_call(second_kernel, out_shape=jax.ShapeDtypeStruct((total, slab...  23.7 us
    all_to_all x2, starting transfers between devices, shards(): lax.all_to_all(part.reshape(2 * parts, frames, slab, 128), ('layer', 'mod...  20.3 us
    pallas_call x2, Pallas kernels, scan_call(): pl.pallas_call(scan_kernel, out_shape=(jax.ShapeDtypeStruct((2, steps, 2,...  18.6 us
    ppermute x1, waiting for transfers between devices, shards(): enter = lax.ppermute(last[:, :slab], 'tm', [(0, 1)])  13.4 us
  transfers between devices with their start and end apart: 3, of which 3 were waited for; matrix products, arithmetic and copies ran while one was open for 0% of the time, Pallas kernels for 15%

profile of v1, /device:TPU:1, one launch (start us, length us, event | category | flops | bytes accessed | tf_op | source)
XLA Modules:
  0.0 178.4 jit_solution(7326758964110423087)
XLA Ops:
  0.0 0.8 slice_bitcast_fusion
  0.8 0.1 multiply_cosine_fusion.1
  0.9 0.5 multiply_cosine_fusion
  1.4 0.8 pad_maximum_fusion.eb
  2.2 1.3 broadcast_in_dim.16.ea
  3.5 4.0 %scan.2 = (bf16[2,16,2,80,2048]{4,3,2,1,0:T(8,128)(2,1)}, bf16[2,80,2048]{2,1,0:T(8,128)(2,1)}) custom-call(s32[1]{0:T(128)} %bitcast.1.flag, f32[2,64,2048]{2,1,0:T(8,128)} %bitcast.26, bf16[2,16,64,2048]{3,2,1,0:T(8,128)(2,1)} %bitcast.18, f32[64,2048]{1,0:T(8,128)} %bitcast.22, f32[64,2048]{1,0:T(8,128)} %bitcast.24, ...), custom_call_target="tpu_custom_call" | custom-call | tf_op jit(solution)/shard_map/scan/pallas_call | solution.py:100
  7.5 1.1 slice.11
  8.6 1.3 collective-permute-start
  9.9 13.4 %collective-permute-done.enter = bf16[2,64,2048]{2,1,0:T(8,128)(2,1)S(1)} collective-permute-done((bf16[2,64,2048]{2,1,0:T(8,128)(2,1)S(1)}, bf16[2,64,2048]{2,1,0:T(8,128)(2,1)S(1)}, u32[]{:S(2)}, u32[]{:S(2)}) %collective-permute-start) | collective-permute-done | bytes 524320 | tf_op jit(solution)/shard_map/ppermute | solution.py:235
  23.3 0.0 copy-start
  23.3 0.8 copy-done
  24.1 14.5 %scan.3 = (bf16[2,16,2,80,2048]{4,3,2,1,0:T(8,128)(2,1)}, bf16[2,80,2048]{2,1,0:T(8,128)(2,1)}) custom-call(s32[1]{0:T(128)} %bitcast.flag, bf16[2,64,2048]{2,1,0:T(8,128)(2,1)} %copy-done, bf16[2,16,64,2048]{3,2,1,0:T(8,128)(2,1)} %bitcast.19, f32[64,2048]{1,0:T(8,128)} %bitcast.23, f32[64,2048]{1,0:T(8,128)} %bitcast.25, ...), custom_call_target="tpu_custom_call", output_to_operand_aliasing={{0}: (7, {})} | custom-call | tf_op jit(solution)/shard_map/scan/pallas_call | solution.py:100
  38.6 14.6 %first.3 = bf16[2,32,4,64,128]{4,3,2,1,0:T(8,128)(2,1)} custom-call(bf16[2,1024,2048]{2,1,0:T(8,128)(2,1)} %constant.29.clone.table, bf16[2,2,8,2,80,2048]{5,4,3,2,1,0:T(8,128)(2,1)} %bitcast.16), custom_call_target="tpu_custom_call" | custom-call | flops 8589934592 | bytes 25165824 | tf_op jit(solution)/shard_map/first/pallas_call | solution.py:140
  53.2 11.5 %all-to-all-start.1 = ((bf16[64,4,64,128]{3,2,1,0:T(8,128)(2,1)}), bf16[64,4,64,128]{3,2,1,0:T(8,128)(2,1)}, u32[]{:S(2)}, u32[]{:S(2)}) async-start(bf16[64,4,64,128]{3,2,1,0:T(8,128)(2,1)} %bitcast.21), calls=%async_computation.1 | async-start | bytes 8388608 | tf_op jit(solution)/shard_map/all_to_all | solution.py:242
  64.7 14.6 %first.2 = bf16[2,32,4,64,128]{4,3,2,1,0:T(8,128)(2,1)} custom-call(bf16[2,1024,2048]{2,1,0:T(8,128)(2,1)} %constant.29.clone.table, bf16[2,2,8,2,80,2048]{5,4,3,2,1,0:T(8,128)(2,1)} %bitcast.17), custom_call_target="tpu_custom_call" | custom-call | flops 8589934592 | bytes 25165824 | tf_op jit(solution)/shard_map/first/pallas_call | solution.py:140
  79.3 28.0 %all-to-all-done.1 = bf16[64,4,64,128]{3,2,1,0:T(8,128)(2,1)} async-done(((bf16[64,4,64,128]{3,2,1,0:T(8,128)(2,1)}), bf16[64,4,64,128]{3,2,1,0:T(8,128)(2,1)}, u32[]{:S(2)}, u32[]{:S(2)}) %all-to-all-start.1) | async-done | bytes 4194336 | tf_op jit(solution)/shard_map/all_to_all | solution.py:242
  107.3 8.9 %all-to-all-start = ((bf16[64,4,64,128]{3,2,1,0:T(8,128)(2,1)}), bf16[64,4,64,128]{3,2,1,0:T(8,128)(2,1)}, u32[]{:S(2)}, u32[]{:S(2)}) async-start(bf16[64,4,64,128]{3,2,1,0:T(8,128)(2,1)} %bitcast.20), calls=%async_computation | async-start | bytes 8388608 | tf_op jit(solution)/shard_map/all_to_all | solution.py:242
  116.2 11.9 %second.2.rest_0_ = f32[8,64,2048]{2,1,0:T(8,128)} custom-call(bf16[4096,2048]{1,0:T(8,128)(2,1)} %constant.30.clone.table, bf16[2,32,4,64,128]{4,3,2,1,0:T(8,128)(2,1)} %bitcast.13.got), custom_call_target="tpu_custom_call" | custom-call | flops 4294967296 | bytes 25165824 | tf_op jit(solution)/shard_map/second/pallas_call | solution.py:191
  128.0 38.6 %all-to-all-done = bf16[64,4,64,128]{3,2,1,0:T(8,128)(2,1)} async-done(((bf16[64,4,64,128]{3,2,1,0:T(8,128)(2,1)}), bf16[64,4,64,128]{3,2,1,0:T(8,128)(2,1)}, u32[]{:S(2)}, u32[]{:S(2)}) %all-to-all-start) | async-done | bytes 4194336 | tf_op jit(solution)/shard_map/all_to_all | solution.py:242
  166.6 11.8 %second.3 = f32[8,64,2048]{2,1,0:T(8,128)} custom-call(bf16[4096,2048]{1,0:T(8,128)(2,1)} %constant.30.clone.table, bf16[2,32,4,64,128]{4,3,2,1,0:T(8,128)(2,1)} %bitcast.11.got, f32[8,64,2048]{2,1,0:T(8,128)} %second.2.rest_0_), custom_call_target="tpu_custom_call", output_to_operand_aliasing={{}: (2, {})} | custom-call | flops 4294967296 | bytes 25165824 | tf_op jit(solution)/shard_map/second/pallas_call | solution.py:191
  (3 shorter events, 0.0 us)
Async XLA Ops:
  8.6 14.7 %collective-permute-start = (bf16[2,64,2048]{2,1,0:T(8,128)(2,1)S(1)}, bf16[2,64,2048]{2,1,0:T(8,128)(2,1)S(1)}, u32[]{:S(2)}, u32[]{:S(2)}) collective-permute-start(bf16[2,64,2048]{2,1,0:T(8,128)(2,1)S(1)} %slice.11), channel_id=1, source_target_pairs={{0,64},{1,65},{2,66},{3,67},{4,68},{5,69},{6,70},{7,71},{8,72},{9,... | collective-permute-start | bytes 1572872 | tf_op jit(solution)/shard_map/ppermute | solution.py:235
  23.3 0.8 copy-start
  53.2 54.1 %all-to-all-start.1 = ((bf16[64,4,64,128]{3,2,1,0:T(8,128)(2,1)}), bf16[64,4,64,128]{3,2,1,0:T(8,128)(2,1)}, u32[]{:S(2)}, u32[]{:S(2)}) async-start(bf16[64,4,64,128]{3,2,1,0:T(8,128)(2,1)} %bitcast.21), calls=%async_computation.1 | async-start | bytes 8388608 | tf_op jit(solution)/shard_map/all_to_all | solution.py:242
  107.3 59.3 %all-to-all-start = ((bf16[64,4,64,128]{3,2,1,0:T(8,128)(2,1)}), bf16[64,4,64,128]{3,2,1,0:T(8,128)(2,1)}, u32[]{:S(2)}, u32[]{:S(2)}) async-start(bf16[64,4,64,128]{3,2,1,0:T(8,128)(2,1)} %bitcast.20), calls=%async_computation | async-start | bytes 8388608 | tf_op jit(solution)/shard_map/all_to_all | solution.py:242

commit v2 on v1

v2 whole, which is shorter than its diff:
```python
import math

import jax
import jax.numpy as jnp
import numpy as np
from jax import lax
from jax.experimental import pallas as pl
from jax.experimental.pallas import tpu as pltpu
from jax.sharding import PartitionSpec as P

F32, BF16 = jnp.float32, jnp.bfloat16
ROWS = 16
FOLD = 4
CHUNKS = 2
VMEM = 56 * 1024 * 1024


def tables(n, parts):
    k = np.arange(n, dtype=np.int64)
    prod = (k[:, None] * k[None, :]) % n
    ang = np.arange(n, dtype=np.float64) * (2.0 * math.pi / n)
    cos, sin = np.cos(ang)[prod], np.sin(ang)[prod]
    depth, slab = n // FOLD, n // parts
    c, s = cos[:, :depth], sin[:, :depth]
    first = np.stack([np.concatenate([c, -s], 1), np.concatenate([s, c], 1)])
    first = first.reshape(2, n // FOLD, FOLD, 2 * depth).transpose(2, 0, 1, 3)
    both = np.stack([cos[:, : n // 2], -sin[:, : n // 2]]) * (1.0 / n)
    both = both.reshape(2, parts, slab // 2, 2, n // 2).transpose(3, 1, 0, 2, 4)
    second = both.reshape(2, n, n // 2)
    order = np.zeros((2, 2, 2, slab, 2, 2, 2, slab // 2))
    for m in range(2):
        for r in range(2):
            for a in range(slab):
                order[m, :, r, a, a % 2, m, r, a // 2] = 1.0
    order = order.reshape(8 * slab, 4 * slab)
    return first.astype(BF16), second.astype(BF16), order.astype(BF16)


def scan_kernel(flag, enter, noise, keep, filt, ca, sa, cb, sb, *rest):
    z, last, ea = rest[-3:]
    steps, slab, n = noise.shape[1:]
    depth = n // FOLD

    def block(enter, noise, keep, filt, ca, sa, z, last):
        for t in range(steps):
            ea[0, t] = jnp.broadcast_to(ca[:, t : t + 1], (ROWS, 128))
            ea[1, t] = jnp.broadcast_to(sa[:, t : t + 1], (ROWS, 128))

        def lanes(j, carry):
            at = [pl.ds(pl.multiple_of(j * 128 + h * depth, 128), 128) for h in range(FOLD)]
            re = [enter[0, :, c].astype(F32) for c in at]
            im = [enter[1, :, c].astype(F32) for c in at]
            for t in range(steps):
                ar, ai = ea[0, t], ea[1, t]
                tr, ti = [], []
                for h in range(FOLD):
                    br, bi = cb[t : t + 1, at[h]], sb[t : t + 1, at[h]]
                    kp, ft = keep[:, at[h]], filt[:, at[h]]
                    gr = kp * (ar * br - ai * bi)
                    gi = kp * (ar * bi + ai * br)
                    nr = gr * re[h] - gi * im[h] + noise[0, t, :, at[h]].astype(F32)
                    ni = gr * im[h] + gi * re[h] + noise[1, t, :, at[h]].astype(F32)
                    re[h], im[h] = nr, ni
                    tr.append((ft * nr).astype(BF16))
                    ti.append((ft * ni).astype(BF16))
                sr, si = tr[0] + tr[2], ti[0] + ti[2]
                dr, di = tr[0] - tr[2], ti[0] - ti[2]
                ur, ui = tr[1] + tr[3], ti[1] + ti[3]
                vr, vi = tr[1] - tr[3], ti[1] - ti[3]
                z[0, t, :, at[0]], z[0, t, :, at[1]] = sr + ur, si + ui
                z[1, t, :, at[0]], z[1, t, :, at[1]] = dr - vi, di + vr
                z[2, t, :, at[0]], z[2, t, :, at[1]] = sr - ur, si - ui
                z[3, t, :, at[0]], z[3, t, :, at[1]] = dr + vi, di - vr
            for h in range(FOLD):
                last[0, :, at[h]] = re[h].astype(BF16)
                last[1, :, at[h]] = im[h].astype(BF16)
            return carry

        lax.fori_loop(0, depth // 128, lanes, 0)

    @pl.when(flag[0] == 1)
    def _():
        pltpu.emit_pipeline(
            block,
            grid=(slab // ROWS,),
            in_specs=[
                pl.BlockSpec((2, ROWS, n), lambda i: (0, i, 0)),
                pl.BlockSpec((2, steps, ROWS, n), lambda i: (0, 0, i, 0)),
                pl.BlockSpec((ROWS, n), lambda i: (i, 0)),
                pl.BlockSpec((ROWS, n), lambda i: (i, 0)),
                pl.BlockSpec((ROWS, steps), lambda i: (i, 0)),
                pl.BlockSpec((ROWS, steps), lambda i: (i, 0)),
            ],
            out_specs=[
                pl.BlockSpec((FOLD, steps, ROWS, 2 * depth), lambda i: (0, 0, i, 0)),
                pl.BlockSpec((2, ROWS, n), lambda i: (0, i, 0)),
            ],
        )(enter, noise, keep, filt, ca, sa, z, last)


def scan_call(flag, enter, noise, keep, filt, ca, sa, cb, sb, z=None):
    steps, slab, n = noise.shape[1:]
    anywhere = pl.BlockSpec(memory_space=pl.ANY)
    inside = pl.BlockSpec(memory_space=pltpu.VMEM)
    in_specs = [pl.BlockSpec(memory_space=pltpu.SMEM)] + [anywhere] * 6 + [inside] * 2
    args = [flag, enter, noise, keep, filt, ca, sa, cb, sb]
    alias = {}
    if z is not None:
        in_specs.append(anywhere)
        args.append(z)
        alias = {9: 0}
    return pl.pallas_call(
        scan_kernel,
        out_shape=(
            jax.ShapeDtypeStruct((FOLD, steps, slab, 2 * n // FOLD), BF16),
            jax.ShapeDtypeStruct((2, slab, n), BF16),
        ),
        in_specs=in_specs,
        out_specs=[anywhere, anywhere],
        scratch_shapes=[pltpu.VMEM((2, steps, ROWS, 128), F32)],
        input_output_aliases=alias,
        compiler_params=pltpu.CompilerParams(vmem_limit_bytes=VMEM),
        name="scan",
    )(*args)


def first_kernel(table, z, out):
    owners, parts, frames, rows = out.shape[:4]
    slab, depth = z.shape[3:]
    left = table[0].reshape(2 * parts * rows, depth)
    right = z[0].reshape(owners * frames * slab, depth)
    acc = lax.dot_general(
        left, right, (((1,), (1,)), ((), ())), preferred_element_type=F32
    ).astype(BF16)
    re, im = acc[: parts * rows], acc[parts * rows :]
    for o in range(owners):
        for f in range(frames):
            c = (o * frames + f) * slab
            pair = jnp.concatenate([re[:, c : c + slab], im[:, c : c + slab]], axis=1)
            out[o, :, f] = pair.reshape(parts, rows, 2 * slab)


def first_call(table, z, chunk, frames, parts):
    total, slab, depth = z.shape[2:]
    rows = slab // FOLD
    return pl.pallas_call(
        first_kernel,
        out_shape=jax.ShapeDtypeStruct((2, parts, frames, slab, 2 * slab), BF16),
        grid=(FOLD,),
        in_specs=[
            pl.BlockSpec((1, 2, parts * rows, depth), lambda i: (i, 0, 0, 0)),
            pl.BlockSpec((1, 2, frames, slab, depth), lambda i: (i, 0, chunk, 0, 0)),
        ],
        out_specs=pl.BlockSpec((2, parts, frames, rows, 2 * slab), lambda i: (0, 0, 0, i, 0)),
        compiler_params=pltpu.CompilerParams(vmem_limit_bytes=VMEM),
        cost_estimate=pl.CostEstimate(
            flops=16 * frames * parts * slab * slab * depth,
            bytes_accessed=16 << 20,
            transcendentals=0,
        ),
        name="first",
    )(table, z)


def second_kernel(table, order, got, *rest):
    out, left, rows = rest[-3:]
    parts, frames, slab, lanes = got.shape[1:]
    piece = slab // FOLD
    tile = table.shape[2]
    half = out.shape[2] // 2
    step = pl.program_id(0)

    @pl.when(step == 0)
    def _():
        for m in range(0, parts, 2):
            four = [got[l, m + k].reshape(frames * slab, lanes) for k in range(2) for l in range(2)]
            both = jnp.dot(
                jnp.concatenate(four, axis=1), order[...], preferred_element_type=F32
            )
            for p in range(2):
                slot = (m + p) % 4
                for f in range(frames):
                    for q in range(FOLD):
                        a = f * slab + q * piece
                        rows[slot, pl.ds(f * slab + q, piece, stride=FOLD), :] = both[
                            a : a + piece, p * lanes : (p + 1) * lanes
                        ]
                left[p, :, m * slab : (m + 2) * slab] = rows[slot].astype(BF16)

    even = jnp.dot(left[0], table[0], preferred_element_type=F32)
    odd = jnp.dot(left[1], table[1], preferred_element_type=F32)
    lo = pl.multiple_of(step * tile, tile)
    out[:, :, pl.ds(lo, tile)] = (even + odd).reshape(frames, slab, tile)
    out[:, :, pl.ds(pl.multiple_of(lo + half, tile), tile)] = (even - odd).reshape(
        frames, slab, tile
    )


def second_call(table, order, got, chunk, total, out=None):
    parts, frames, slab = got.shape[1:4]
    depth, half = table.shape[1:]
    tile = 256
    in_specs = [
        pl.BlockSpec((2, depth, tile), lambda i: (0, 0, i)),
        pl.BlockSpec(order.shape, lambda i: (0, 0)),
        pl.BlockSpec(got.shape, lambda i: (0, 0, 0, 0, 0)),
    ]
    args = [table, order, got]
    alias = {}
    if out is not None:
        in_specs.append(pl.BlockSpec(memory_space=pl.ANY))
        args.append(out)
        alias = {3: 0}
    return pl.pallas_call(
        second_kernel,
        out_shape=jax.ShapeDtypeStruct((total, slab, 2 * half), F32),
        grid=(half // tile,),
        in_specs=in_specs,
        out_specs=pl.BlockSpec((frames, slab, 2 * half), lambda i: (chunk, 0, 0)),
        scratch_shapes=[
            pltpu.VMEM((2, frames * slab, depth), BF16),
            pltpu.VMEM((4, frames * slab, 2 * slab), F32),
        ],
        input_output_aliases=alias,
        compiler_params=pltpu.CompilerParams(vmem_limit_bytes=VMEM),
        cost_estimate=pl.CostEstimate(
            flops=4 * depth * half * frames * slab, bytes_accessed=16 << 20, transcendentals=0
        ),
        name="second",
    )(*args)


def shards(innovation, retention, rytov_filter, wind_shift, start_state):
    steps, slab, n = innovation.shape[2:]
    noise = innovation.reshape(2, steps, slab, n)
    keep, filt = retention.reshape(slab, n), rytov_filter.reshape(slab, n)
    wind = wind_shift.reshape(steps, 2)
    parts = lax.axis_size("mode")
    total = steps // 2
    frames = total // CHUNKS
    first, second, order = tables(n, parts)

    def waves(k):
        return jnp.where(k >= n // 2, k - n, k).astype(F32)

    angle_step = 2.0 * math.pi / n
    rows = lax.axis_index("mode") * slab + lax.iota(jnp.int32, slab)
    pa = (waves(rows) * angle_step)[:, None] * wind[None, :, 0]
    pb = wind[:, 1:2] * (waves(lax.iota(jnp.int32, n)) * angle_step)[None]
    turns = (jnp.cos(pa), jnp.sin(pa), jnp.cos(pb), jnp.sin(pb))

    core = lax.axis_index("tm").astype(jnp.int32)
    start = start_state.reshape(2, slab, n)
    z, last = scan_call((1 - core)[None], start, noise, keep, filt, *turns)
    enter = lax.ppermute(last, "tm", [(0, 1), (1, 0)])
    z, _ = scan_call(core[None], enter, noise, keep, filt, *turns, z)
    z = z.reshape(FOLD, 2, total, slab, 2 * n // FOLD)

    out = None
    for c in range(CHUNKS):
        part = first_call(first, z, c, frames, parts)
        got = lax.all_to_all(
            part.reshape(2 * parts, frames, slab, 2 * slab), ("layer", "mode"), 0, 0, tiled=True
        ).reshape(2, parts, frames, slab, 2 * slab)
        out = second_call(second, order, got, c, total, out)
    return out


def solution(mesh):
    return jax.shard_map(
        shards,
        mesh=mesh,
        in_specs=(
            P(None, "layer", "tm", "mode", None),
            P("layer", "mode", None),
            P("layer", "mode", None),
            P("layer", "tm", None),
            P(None, "layer", "mode", None),
        ),
        out_specs=P(("tm", "layer"), "mode", None),
        check_vma=False,
    )
```

time: 180 us -> 176 us (0.978)
  Pallas kernels: 71.4 us -> 52.4 us
  starting transfers between devices: 21.6 us -> 33.2 us
  waiting for transfers between devices: 80 us -> 86.3 us
  local copies, waits for them, and re-layouts: 3.94 us -> 1.55 us
    all_to_all x2, waiting for transfers between devices: 66.6 us -> 84.6 us  [shards(): lax.all_to_all(part.reshape(2 * parts, frames, slab, 2 * slab), ('layer',...]
    ppermute x1, starting transfers between devices: 1.29 us -> 13.4 us  [shards(): enter = lax.ppermute(last, 'tm', [(0, 1), (1, 0)])]
    ppermute x1, waiting for transfers between devices: 13.4 us -> 1.75 us  [shards(): enter = lax.ppermute(last, 'tm', [(0, 1), (1, 0)])]
    pallas_call x2, Pallas kernels: 29.2 us -> 18.9 us  [first_call(): pl.pallas_call(first_kernel, out_shape=jax.ShapeDtypeStruct((2, parts, fr...]
    pallas_call x2, Pallas kernels: 18.6 us -> 13.9 us  [scan_call(): pl.pallas_call(scan_kernel, out_shape=(jax.ShapeDtypeStruct((FOLD, steps,...]
    pallas_call x2, Pallas kernels: 23.7 us -> 19.5 us  [second_call(): pl.pallas_call(second_kernel, out_shape=jax.ShapeDtypeStruct((total, slab...]
    sin x0 -> x2, other arithmetic: none -> 2.09 us  [shards(): turns = (jnp.cos(pa), jnp.sin(pa), jnp.cos(pb), jnp.sin(pb))]
  transfers between devices with their start and end apart: 3 -> 3, of which waited for: 3 -> 3; matrix products, arithmetic and copies ran while one was open for 0% -> 0% of each run, Pallas kernels for 15% -> 11%
where the time goes in v2:
time: 176 us
  waiting for transfers between devices  86.3 us (49%)
  Pallas kernels  52.4 us (30%)
  starting transfers between devices  33.2 us (19%)
  other arithmetic  2.11 us (1%)
    all_to_all x2, waiting for transfers between devices, shards(): lax.all_to_all(part.reshape(2 * parts, frames, slab, 2 * slab), ('layer',...  84.6 us
    all_to_all x2, starting transfers between devices, shards(): lax.all_to_all(part.reshape(2 * parts, frames, slab, 2 * slab), ('layer',...  19.8 us
    pallas_call x2, Pallas kernels, second_call(): pl.pallas_call(second_kernel, out_shape=jax.ShapeDtypeStruct((total, slab...  19.5 us
    pallas_call x2, Pallas kernels, first_call(): pl.pallas_call(first_kernel, out_shape=jax.ShapeDtypeStruct((2, parts, fr...  18.9 us
    pallas_call x2, Pallas kernels, scan_call(): pl.pallas_call(scan_kernel, out_shape=(jax.ShapeDtypeStruct((FOLD, steps,...  13.9 us
    ppermute x1, starting transfers between devices, shards(): enter = lax.ppermute(last, 'tm', [(0, 1), (1, 0)])  13.4 us
  transfers between devices with their start and end apart: 3, of which 3 were waited for; matrix products, arithmetic and copies ran while one was open for 0% of the time, Pallas kernels for 11%

profile of v2, /device:TPU:1, one launch (start us, length us, event | category | flops | bytes accessed | tf_op | source)
XLA Modules:
  0.0 175.6 jit_solution(11875088988701557310)
XLA Ops:
  0.0 0.8 slice_bitcast_fusion
  0.8 0.8 multiply_sine_fusion.1
  1.6 1.3 multiply_sine_fusion
  2.9 1.0 scan.2
  3.8 13.4 %collective-permute-start = (bf16[2,64,2048]{2,1,0:T(8,128)(2,1)}, bf16[2,64,2048]{2,1,0:T(8,128)(2,1)S(1)}, u32[]{:S(2)}, u32[]{:S(2)}) collective-permute-start(bf16[2,64,2048]{2,1,0:T(8,128)(2,1)} %get-tuple-element.8), channel_id=1, source_target_pairs={{0,64},{64,0},{1,65},{65,1},{2,66},{66,2},{3,67},{67,3},{4,68},{68... | collective-permute-start | bytes 1572872 | tf_op jit(solution)/shard_map/ppermute | solution.py:255
  17.2 1.7 collective-permute-done.enter
  19.0 0.0 copy-start
  19.0 0.8 copy-done
  19.8 13.0 %scan.3 = (bf16[4,16,64,1024]{3,2,1,0:T(8,128)(2,1)}, bf16[2,64,2048]{2,1,0:T(8,128)(2,1)}) custom-call(s32[1]{0:T(128)} %bitcast.flag, bf16[2,64,2048]{2,1,0:T(8,128)(2,1)} %copy-done, bf16[2,16,64,2048]{3,2,1,0:T(8,128)(2,1)} %bitcast.17, f32[64,2048]{1,0:T(8,128)} %bitcast.23, f32[64,2048]{1,0:T(8,128)} %bitcast.25, ...), custom_call_target="tpu_custom_call", output_to_operand_aliasing={{0}: (9, {})} | custom-call | tf_op jit(solution)/shard_map/scan/pallas_call | solution.py:112
  32.7 9.4 %first.3 = bf16[2,32,4,64,128]{4,3,2,1,0:T(8,128)(2,1)} custom-call(bf16[4,2,512,1024]{3,2,1,0:T(8,128)(2,1)} %constant.31.clone.table, bf16[4,2,8,64,1024]{4,3,2,1,0:T(8,128)(2,1)} %bitcast.18), custom_call_target="tpu_custom_call" | custom-call | flops 8589934592 | bytes 16777216 | tf_op jit(solution)/shard_map/first/pallas_call | solution.py:146
  42.1 11.5 %all-to-all-start.1 = ((bf16[64,4,64,128]{3,2,1,0:T(8,128)(2,1)}), bf16[64,4,64,128]{3,2,1,0:T(8,128)(2,1)}, u32[]{:S(2)}, u32[]{:S(2)}) async-start(bf16[64,4,64,128]{3,2,1,0:T(8,128)(2,1)} %bitcast.21), calls=%async_computation.1 | async-start | bytes 8388608 | tf_op jit(solution)/shard_map/all_to_all | solution.py:262
  53.6 9.5 %first.2 = bf16[2,32,4,64,128]{4,3,2,1,0:T(8,128)(2,1)} custom-call(bf16[4,2,512,1024]{3,2,1,0:T(8,128)(2,1)} %constant.31.clone.table, bf16[4,2,8,64,1024]{4,3,2,1,0:T(8,128)(2,1)} %bitcast.19), custom_call_target="tpu_custom_call" | custom-call | flops 8589934592 | bytes 16777216 | tf_op jit(solution)/shard_map/first/pallas_call | solution.py:146
  63.1 31.5 %all-to-all-done.1 = bf16[64,4,64,128]{3,2,1,0:T(8,128)(2,1)} async-done(((bf16[64,4,64,128]{3,2,1,0:T(8,128)(2,1)}), bf16[64,4,64,128]{3,2,1,0:T(8,128)(2,1)}, u32[]{:S(2)}, u32[]{:S(2)}) %all-to-all-start.1) | async-done | bytes 4194336 | tf_op jit(solution)/shard_map/all_to_all | solution.py:262
  94.6 8.4 %all-to-all-start = ((bf16[64,4,64,128]{3,2,1,0:T(8,128)(2,1)}), bf16[64,4,64,128]{3,2,1,0:T(8,128)(2,1)}, u32[]{:S(2)}, u32[]{:S(2)}) async-start(bf16[64,4,64,128]{3,2,1,0:T(8,128)(2,1)} %bitcast.20), calls=%async_computation | async-start | bytes 8388608 | tf_op jit(solution)/shard_map/all_to_all | solution.py:262
  103.0 9.8 %second.2.rest_0_ = f32[8,64,2048]{2,1,0:T(8,128)} custom-call(bf16[2,2048,1024]{2,1,0:T(8,128)(2,1)} %constant.32.clone.table, bf16[512,256]{1,0:T(8,128)(2,1)} %constant.33.clone.order, bf16[2,32,4,64,128]{4,3,2,1,0:T(8,128)(2,1)} %bitcast.13.got), custom_call_target="tpu_custom_call" | custom-call | flops 2147483648 | bytes 16777216 | tf_op jit(solution)/shard_map/second/pallas_call | solution.py:214
  112.7 53.1 %all-to-all-done = bf16[64,4,64,128]{3,2,1,0:T(8,128)(2,1)} async-done(((bf16[64,4,64,128]{3,2,1,0:T(8,128)(2,1)}), bf16[64,4,64,128]{3,2,1,0:T(8,128)(2,1)}, u32[]{:S(2)}, u32[]{:S(2)}) %all-to-all-start) | async-done | bytes 4194336 | tf_op jit(solution)/shard_map/all_to_all | solution.py:262
  165.9 9.7 %second.3 = f32[8,64,2048]{2,1,0:T(8,128)} custom-call(bf16[2,2048,1024]{2,1,0:T(8,128)(2,1)} %constant.32.clone.table, bf16[512,256]{1,0:T(8,128)(2,1)} %constant.33.clone.order, bf16[2,32,4,64,128]{4,3,2,1,0:T(8,128)(2,1)} %bitcast.11.got, f32[8,64,2048]{2,1,0:T(8,128)} %second.2.rest_0_), custom_call_target="tpu_custom_call", output_to_operand_aliasing={{}: (3, {})} | custom-call | flops 2147483648 | bytes 16777216 | tf_op jit(solution)/shard_map/second/pallas_call | solution.py:214
  (2 shorter events, 0.0 us)
Async XLA Ops:
  3.8 15.1 %collective-permute-start = (bf16[2,64,2048]{2,1,0:T(8,128)(2,1)}, bf16[2,64,2048]{2,1,0:T(8,128)(2,1)S(1)}, u32[]{:S(2)}, u32[]{:S(2)}) collective-permute-start(bf16[2,64,2048]{2,1,0:T(8,128)(2,1)} %get-tuple-element.8), channel_id=1, source_target_pairs={{0,64},{64,0},{1,65},{65,1},{2,66},{66,2},{3,67},{67,3},{4,68},{68... | collective-permute-start | bytes 1572872 | tf_op jit(solution)/shard_map/ppermute | solution.py:255
  19.0 0.8 copy-start
  42.1 52.4 %all-to-all-start.1 = ((bf16[64,4,64,128]{3,2,1,0:T(8,128)(2,1)}), bf16[64,4,64,128]{3,2,1,0:T(8,128)(2,1)}, u32[]{:S(2)}, u32[]{:S(2)}) async-start(bf16[64,4,64,128]{3,2,1,0:T(8,128)(2,1)} %bitcast.21), calls=%async_computation.1 | async-start | bytes 8388608 | tf_op jit(solution)/shard_map/all_to_all | solution.py:262
  94.6 71.3 %all-to-all-start = ((bf16[64,4,64,128]{3,2,1,0:T(8,128)(2,1)}), bf16[64,4,64,128]{3,2,1,0:T(8,128)(2,1)}, u32[]{:S(2)}, u32[]{:S(2)}) async-start(bf16[64,4,64,128]{3,2,1,0:T(8,128)(2,1)} %bitcast.20), calls=%async_computation | async-start | bytes 8388608 | tf_op jit(solution)/shard_map/all_to_all | solution.py:262

commit v3 on v2

v3 whole, which is shorter than its diff:
```python
import functools
import math

import jax
import jax.numpy as jnp
import numpy as np
from jax import lax
from jax.experimental import pallas as pl
from jax.experimental.pallas import tpu as pltpu
from jax.sharding import PartitionSpec as P

F32, BF16 = jnp.float32, jnp.bfloat16
ROWS = 16
FOLD = 4
CLASSES = 8
SPAN = 4
VMEM = 56 * 1024 * 1024


def tables(n, parts):
    k = np.arange(n, dtype=np.int64)
    prod = (k[:, None] * k[None, :]) % n
    ang = np.arange(n, dtype=np.float64) * (2.0 * math.pi / n)
    cos, sin = np.cos(ang)[prod], np.sin(ang)[prod]
    depth, slab = n // CLASSES, n // parts
    c, s = cos[:, :depth], sin[:, :depth]
    first = np.stack([np.concatenate([c, -s], 1), np.concatenate([s, c], 1)])
    first = first.reshape(2, n // CLASSES, CLASSES, 2 * depth).transpose(2, 0, 1, 3)
    both = np.stack([cos[:, : n // 2], -sin[:, : n // 2]]) * (1.0 / n)
    both = both.reshape(2, parts, slab // 2, 2, n // 2).transpose(3, 1, 0, 2, 4)
    second = both.reshape(2, n, n // 2)
    order = np.zeros((2, 2, slab, 2, 2, 2, slab // 2))
    for m in range(2):
        for r in range(2):
            for a in range(slab):
                order[m, r, a, a % 2, m, r, a // 2] = 1.0
    order = order.reshape(4 * slab, 4 * slab)
    return first.astype(BF16), second.astype(BF16), order.astype(BF16)


def wave_kernel(direct, flag, wind, enter, noise, keep, filt, table, *rest):
    (
        part, last, enter_v, noise_v, keep_v, filt_v, table_v, part_v, last_v,
        ea, cb, sb, state, z, zz, sems,
    ) = rest[-16:]
    steps, slab, n = noise.shape[1:]
    parts, frames = part.shape[1], part.shape[3]
    depth = n // FOLD
    blocks = steps // SPAN
    entry = enter if direct else enter_v

    def noise_copy(i):
        at = pl.ds(i * SPAN, SPAN)
        return pltpu.make_async_copy(noise.at[:, at], noise_v.at[:, at], sems.at[4 + i])

    def part_copy(q):
        return pltpu.make_async_copy(part_v.at[q], part.at[:, :, q], sems.at[4 + blocks + q])

    def scan(i, rb):
        rows = pl.ds(pl.multiple_of(rb * ROWS, ROWS), ROWS)
        for j in range(depth // 128):
            at = [slice(j * 128 + h * depth, j * 128 + h * depth + 128) for h in range(FOLD)]
            if i == 0:
                re = [entry[0, rows, c].astype(F32) for c in at]
                im = [entry[1, rows, c].astype(F32) for c in at]
            else:
                re = [state[0, rows, c] for c in at]
                im = [state[1, rows, c] for c in at]
            for s in range(SPAN):
                t = i * SPAN + s
                ar, ai = ea[0, t, rows], ea[1, t, rows]
                tr, ti = [], []
                for h in range(FOLD):
                    br, bi = cb[t : t + 1, at[h]], sb[t : t + 1, at[h]]
                    kp, ft = keep_v[rows, at[h]], filt_v[rows, at[h]]
                    gr = kp * (ar * br - ai * bi)
                    gi = kp * (ar * bi + ai * br)
                    nr = gr * re[h] - gi * im[h] + noise_v[0, t, rows, at[h]].astype(F32)
                    ni = gr * im[h] + gi * re[h] + noise_v[1, t, rows, at[h]].astype(F32)
                    re[h], im[h] = nr, ni
                    tr.append((ft * nr).astype(BF16))
                    ti.append((ft * ni).astype(BF16))
                sr, si = tr[0] + tr[2], ti[0] + ti[2]
                dr, di = tr[0] - tr[2], ti[0] - ti[2]
                ur, ui = tr[1] + tr[3], ti[1] + ti[3]
                vr, vi = tr[1] - tr[3], ti[1] - ti[3]
                z[0, t, rows, at[0]], z[0, t, rows, at[1]] = sr + ur, si + ui
                z[1, t, rows, at[0]], z[1, t, rows, at[1]] = dr - vi, di + vr
                z[2, t, rows, at[0]], z[2, t, rows, at[1]] = sr - ur, si - ui
                z[3, t, rows, at[0]], z[3, t, rows, at[1]] = dr + vi, di - vr
            for h in range(FOLD):
                if i < blocks - 1:
                    state[0, rows, at[h]], state[1, rows, at[h]] = re[h], im[h]
                else:
                    last_v[0, rows, at[h]] = re[h].astype(BF16)
                    last_v[1, rows, at[h]] = im[h].astype(BF16)

    def turns():
        angle = 2.0 * math.pi / n
        lane = lax.broadcasted_iota(jnp.int32, (slab, 128), 1)
        line = lax.broadcasted_iota(jnp.int32, (slab, 128), 0)
        across = jnp.zeros((slab, 128), F32)
        down = jnp.zeros((steps, 128), F32)
        for t in range(steps):
            across = jnp.where(lane == t, wind[0, t], across)
            down = jnp.where(line[:steps] == t, wind[1, t], down)

        def waves(k):
            return jnp.where(k >= n // 2, k - n, k).astype(F32) * angle

        pa = waves(line + flag[1]) * across
        fine = lane[:steps].astype(F32) * angle * down
        coarse = waves(lane[:steps] * 128) * down
        ca, sa = jnp.cos(pa), jnp.sin(pa)
        cq, sq = jnp.cos(fine), jnp.sin(fine)
        cp, sp = jnp.cos(coarse), jnp.sin(coarse)
        for t in range(steps):
            ea[0, t] = jnp.broadcast_to(ca[:, t : t + 1], (slab, 128))
            ea[1, t] = jnp.broadcast_to(sa[:, t : t + 1], (slab, 128))
        for c in range(n // 128):
            x, y = cp[:, c : c + 1], sp[:, c : c + 1]
            cb[:, c * 128 : (c + 1) * 128] = x * cq - y * sq
            sb[:, c * 128 : (c + 1) * 128] = x * sq + y * cq

    def fold(q):
        quarter = depth // 2
        root = jnp.asarray(math.sqrt(0.5), BF16)
        for t in range(steps):
            rows = pl.ds(t * slab, slab)
            lr, hr, li, hi = (z[q, t, :, k * quarter : (k + 1) * quarter] for k in range(4))
            if q == 0:
                wr, wi = hr, hi
            elif q == 1:
                wr, wi = (hr - hi) * root, (hr + hi) * root
            elif q == 2:
                wr, wi = -hi, hr
            else:
                wr, wi = -(hr + hi) * root, (hr - hi) * root
            zz[0, rows, :quarter], zz[0, rows, quarter:] = lr + wr, li + wi
            zz[1, rows, :quarter], zz[1, rows, quarter:] = lr - wr, li - wi

    def transform(q):
        piece = slab // CLASSES
        left = [table_v[q + FOLD * p].reshape(2 * parts * piece, depth) for p in range(2)]
        acc = [
            lax.dot_general(
                left[p], zz[p], (((1,), (1,)), ((), ())), preferred_element_type=F32
            )
            for p in range(2)
        ]
        for o in range(2):
            for f in range(frames):
                c = (o * frames + f) * slab
                both = []
                for p in range(2):
                    re, im = acc[p][: parts * piece], acc[p][parts * piece :]
                    pair = jnp.concatenate([re[:, c : c + slab], im[:, c : c + slab]], axis=1)
                    both.append(pair.reshape(parts, piece, 2 * slab))
                part_v[q, o, :, f] = jnp.concatenate(both, axis=1).astype(BF16)

    @pl.when(flag[0] == 1)
    def _():
        heads = [
            pltpu.make_async_copy(keep, keep_v, sems.at[1]),
            pltpu.make_async_copy(filt, filt_v, sems.at[2]),
        ]
        if not direct:
            heads.append(pltpu.make_async_copy(enter, enter_v, sems.at[0]))
        full = pltpu.make_async_copy(table, table_v, sems.at[3])
        for c in heads:
            c.start()
        noise_copy(0).start()
        noise_copy(1).start()
        full.start()
        for i in range(2, blocks):
            noise_copy(i).start()
        turns()
        for c in heads:
            c.wait()
        for i in range(blocks):
            noise_copy(i).wait()

            def piece(rb, carry):
                scan(i, rb)
                return carry

            lax.fori_loop(0, slab // ROWS, piece, 0)
        final = pltpu.make_async_copy(last_v, last, sems.at[0])
        final.start()
        full.wait()

        for q in range(FOLD):
            fold(q)
            transform(q)
            part_copy(q).start()
        final.wait()
        for q in range(FOLD):
            part_copy(q).wait()


def wave_call(flag, wind, enter, noise, keep, filt, table, parts, part=None):
    steps, slab, n = noise.shape[1:]
    direct = part is not None
    anywhere = pl.BlockSpec(memory_space=pl.ANY)
    inside = pl.BlockSpec(memory_space=pltpu.VMEM)
    scalars = pl.BlockSpec(memory_space=pltpu.SMEM)
    in_specs = [scalars, scalars, inside if direct else anywhere] + [anywhere] * 4
    args = [flag, wind, enter, noise, keep, filt, table]
    alias = {}
    if direct:
        in_specs.append(anywhere)
        args.append(part)
        alias = {7: 0}
    blocks = steps // SPAN
    piece = slab // FOLD
    depth = n // FOLD
    return pl.pallas_call(
        functools.partial(wave_kernel, direct),
        out_shape=(
            jax.ShapeDtypeStruct((2, parts, FOLD, steps // 2, piece, 2 * slab), BF16),
            jax.ShapeDtypeStruct((2, slab, n), BF16),
        ),
        in_specs=in_specs,
        out_specs=[anywhere, anywhere],
        scratch_shapes=[
            pltpu.VMEM((2, 8, 128) if direct else enter.shape, enter.dtype),
            pltpu.VMEM(noise.shape, noise.dtype),
            pltpu.VMEM(keep.shape, F32),
            pltpu.VMEM(filt.shape, F32),
            pltpu.VMEM(table.shape, BF16),
            pltpu.VMEM((FOLD, 2, parts, steps // 2, piece, 2 * slab), BF16),
            pltpu.VMEM((2, slab, n), BF16),
            pltpu.VMEM((2, steps, slab, 128), F32),
            pltpu.VMEM((steps, n), F32),
            pltpu.VMEM((steps, n), F32),
            pltpu.VMEM((2, slab, n), F32),
            pltpu.VMEM((FOLD, steps, slab, 2 * depth), BF16),
            pltpu.VMEM((2, steps * slab, depth), BF16),
            pltpu.SemaphoreType.DMA((4 + blocks + FOLD,)),
        ],
        input_output_aliases=alias,
        compiler_params=pltpu.CompilerParams(vmem_limit_bytes=VMEM),
        name="wave",
    )(*args)


TILE = 512
GATHER = 2


def second_kernel(start, table, order, got, *rest):
    out, left, done, sems = rest[-4:]
    parts, _, frames, piece, lanes = got.shape[1:]
    slab = FOLD * piece
    tile = table.shape[2]
    half = out.shape[2] // 2
    step = pl.program_id(0)

    @pl.when(step < GATHER)
    def _():
        for m in range(0, parts, 2):
            two = [(got[0, m + k] + got[1, m + k]).reshape(frames * slab, lanes) for k in range(2)]
            both = jnp.dot(
                jnp.concatenate(two, axis=1), order[...], preferred_element_type=F32
            )
            at = pl.multiple_of((step * parts + m) * slab, lanes)
            for p in range(2):
                left[p, :, pl.ds(at, lanes)] = both[:, p * lanes : (p + 1) * lanes].astype(BF16)

    def copy(i, h, w):
        lo = pl.multiple_of(i * tile + h * half + w * lanes, lanes)
        return pltpu.make_async_copy(
            done.at[h, i, w], out.at[pl.ds(start, frames), :, pl.ds(lo, lanes)], sems.at[h, i, w]
        )

    tiles = half // tile

    @pl.when(step >= GATHER)
    def _():
        i = step - GATHER
        even = jnp.dot(left[0], table[0], preferred_element_type=F32)
        odd = jnp.dot(left[1], table[1], preferred_element_type=F32)
        for h, both in enumerate((even + odd, even - odd)):
            for w in range(tile // lanes):
                for q in range(FOLD):
                    for f in range(frames):
                        for p in range(2):
                            a = (q * frames + f) * piece + p * piece // 2
                            at = pl.ds(q + FOLD * p, piece // 2, stride=CLASSES)
                            done[h, i, w, f, at, :] = both[
                                a : a + piece // 2, w * lanes : (w + 1) * lanes
                            ]
                copy(i, h, w).start()

    @pl.when(step == GATHER + tiles - 1)
    def _():
        for i in range(tiles):
            for h in range(2):
                for w in range(tile // lanes):
                    copy(i, h, w).wait()


def second_call(table, order, got, start, total, out=None):
    parts, _, frames, piece, lanes = got.shape[1:]
    slab = FOLD * piece
    depth, half = table.shape[1:]
    tile = TILE
    in_specs = [
        pl.BlockSpec((2, depth, tile), lambda i: (0, 0, jnp.maximum(i - GATHER, 0))),
        pl.BlockSpec(order.shape, lambda i: (0, 0)),
        pl.BlockSpec(
            (2, parts // GATHER, FOLD, frames, piece, lanes),
            lambda i: (0, jnp.minimum(i, GATHER - 1), 0, 0, 0, 0),
        ),
    ]
    args = [table, order, got]
    alias = {}
    if out is not None:
        in_specs.append(pl.BlockSpec(memory_space=pl.ANY))
        args.append(out)
        alias = {3: 0}
    return pl.pallas_call(
        functools.partial(second_kernel, start),
        out_shape=jax.ShapeDtypeStruct((total, slab, 2 * half), F32),
        grid=(GATHER + half // tile,),
        in_specs=in_specs,
        out_specs=pl.BlockSpec(memory_space=pl.ANY),
        scratch_shapes=[
            pltpu.VMEM((2, frames * slab, depth), BF16),
            pltpu.VMEM((2, half // tile, tile // lanes, frames, slab, lanes), F32),
            pltpu.SemaphoreType.DMA((2, half // tile, tile // lanes)),
        ],
        input_output_aliases=alias,
        compiler_params=pltpu.CompilerParams(vmem_limit_bytes=VMEM),
        cost_estimate=pl.CostEstimate(
            flops=4 * depth * half * frames * slab, bytes_accessed=20 << 20, transcendentals=0
        ),
        name="second",
    )(*args)


def shards(innovation, retention, rytov_filter, wind_shift, start_state):
    steps, slab, n = innovation.shape[2:]
    noise = innovation.reshape(2, steps, slab, n)
    keep, filt = retention.reshape(slab, n), rytov_filter.reshape(slab, n)
    wind = wind_shift.reshape(steps, 2).T
    parts = lax.axis_size("mode")
    first, second, order = tables(n, parts)

    core = lax.axis_index("tm").astype(jnp.int32)
    row = lax.axis_index("mode").astype(jnp.int32) * slab
    start = start_state.reshape(2, slab, n)
    flags = [jnp.stack([on, row]) for on in (1 - core, core)]
    part, last = wave_call(flags[0], wind, start, noise, keep, filt, first, parts)
    enter = lax.ppermute(last, "tm", [(0, 1), (1, 0)])
    part, _ = wave_call(flags[1], wind, enter, noise, keep, filt, first, parts, part)
    got = lax.all_to_all(
        part.reshape((2 * parts,) + part.shape[2:]), ("layer", "mode"), 0, 0, tiled=True
    ).reshape(part.shape)
    return second_call(second, order, got, 0, steps // 2)


def solution(mesh):
    return jax.shard_map(
        shards,
        mesh=mesh,
        in_specs=(
            P(None, "layer", "tm", "mode", None),
            P("layer", "mode", None),
            P("layer", "mode", None),
            P("layer", "tm", None),
            P(None, "layer", "mode", None),
        ),
        out_specs=P(("tm", "layer"), "mode", None),
        check_vma=False,
    )
```

time: 176 us -> 145 us (0.82)
  blocking collectives: 0 us -> 94.1 us
  waiting for transfers between devices: 86.3 us -> 1.14 us
  Pallas kernels: 52.4 us -> 29.9 us
  starting transfers between devices: 33.2 us -> 17.3 us
    all_to_all x0 -> x1, blocking collectives: none -> 94.1 us  [shards(): lax.all_to_all(part.reshape((2 * parts,) + part.shape[2:]), ('layer', 'mo...]
    all_to_all x2 -> x0, waiting for transfers between devices: 84.6 us -> none  [shards(): lax.all_to_all(part.reshape(2 * parts, frames, slab, 2 * slab), ('layer',...]
    pallas_call x6 -> x3, Pallas kernels: 52.4 us -> 29.9 us  [the longest x2 17.7 us: wave_call(): pl.pallas_call(functools.partial(wave_kernel, direct), out_shape=(jax.Sha...]
    all_to_all x2 -> x0, starting transfers between devices: 19.8 us -> none  [shards(): lax.all_to_all(part.reshape(2 * parts, frames, slab, 2 * slab), ('layer',...]
    ppermute x1, starting transfers between devices: 13.4 us -> 17.3 us  [shards(): enter = lax.ppermute(last, 'tm', [(0, 1), (1, 0)])]
    sin x2 -> x0, other arithmetic: 2.09 us -> none  [shards(): turns = (jnp.cos(pa), jnp.sin(pa), jnp.cos(pb), jnp.sin(pb))]
  transfers between devices with their start and end apart: 3 -> 1, of which waited for: 3 -> 1; matrix products, arithmetic and copies ran while one was open for 0% -> 0% of each run, Pallas kernels for 11% -> 0%
where the time goes in v3:
time: 145 us
  blocking collectives  94.1 us (65%)
  Pallas kernels  29.9 us (21%)
  starting transfers between devices  17.3 us (12%)
    all_to_all x1, blocking collectives, shards(): lax.all_to_all(part.reshape((2 * parts,) + part.shape[2:]), ('layer', 'mo...  94.1 us
    pallas_call x2, Pallas kernels, wave_call(): pl.pallas_call(functools.partial(wave_kernel, direct), out_shape=(jax.Sha...  17.7 us
    ppermute x1, starting transfers between devices, shards(): enter = lax.ppermute(last, 'tm', [(0, 1), (1, 0)])  17.3 us
    pallas_call x1, Pallas kernels, second_call(): pl.pallas_call(functools.partial(second_kernel, start), out_shape=jax.Sha...  12.3 us
  transfers between devices with their start and end apart: 1, of which 1 were waited for; matrix products, arithmetic and copies ran while one was open for 0% of the time, Pallas kernels for 0%

profile of v3, /device:TPU:1, one launch (start us, length us, event | category | flops | bytes accessed | tf_op | source)
XLA Modules:
  0.0 144.7 jit_solution(6762071129441277868)
XLA Ops:
  0.0 0.6 pad_add_fusion.1.flag
  0.6 0.8 wave.2
  1.5 17.3 %collective-permute-start = (bf16[2,64,2048]{2,1,0:T(8,128)(2,1)}, bf16[2,64,2048]{2,1,0:T(8,128)(2,1)S(1)}, u32[]{:S(2)}, u32[]{:S(2)}) collective-permute-start(bf16[2,64,2048]{2,1,0:T(8,128)(2,1)} %get-tuple-element.8), channel_id=1, source_target_pairs={{0,64},{64,0},{1,65},{65,1},{2,66},{66,2},{3,67},{67,3},{4,68},{68... | collective-permute-start | bytes 1572872 | tf_op jit(solution)/shard_map/ppermute | solution.py:355
  18.8 0.6 pad_add_fusion.flag
  19.4 1.1 collective-permute-done.enter
  20.5 0.0 copy-start
  20.5 0.8 copy-done
  21.3 16.9 %wave.3 = (bf16[2,32,4,8,16,128]{5,4,3,2,1,0:T(8,128)(2,1)}, bf16[2,64,2048]{2,1,0:T(8,128)(2,1)}) custom-call(s32[2]{0:T(128)} %pad_add_fusion.flag, f32[2,16]{1,0:T(2,128)} %bitcast.22, bf16[2,64,2048]{2,1,0:T(8,128)(2,1)} %copy-done, bf16[2,16,64,2048]{3,2,1,0:T(8,128)(2,1)} %bitcast.13, f32[64,2048]{1,0:T(8,128)} %bitcast.17, ...), custom_call_target="tpu_custom_call", output_to_operand_aliasing={{0}: (7, {})} | custom-call | tf_op jit(solution)/shard_map/wave/pallas_call | solution.py:217
  38.2 94.1 %all_to_all.5 = bf16[64,4,8,16,128]{4,3,2,1,0:T(8,128)(2,1)} all-to-all(bf16[64,4,8,16,128]{4,3,2,1,0:T(8,128)(2,1)} %bitcast.14), channel_id=1, replica_groups=mesh['tm'=2,'layer'=2,'mode'=32] {'layer','mode'}, dimensions={0} | all-to-all | bytes 16777216 | tf_op jit(solution)/shard_map/all_to_all | solution.py:357
  132.3 12.3 %second.1 = f32[8,64,2048]{2,1,0:T(8,128)} custom-call(bf16[2,2048,1024]{2,1,0:T(8,128)(2,1)} %constant.21.clone.table, bf16[256,256]{1,0:T(8,128)(2,1)} %constant.22.clone.order, bf16[2,32,4,8,16,128]{5,4,3,2,1,0:T(8,128)(2,1)} %bitcast.15), custom_call_target="tpu_custom_call" | custom-call | flops 4294967296 | bytes 20971520 | tf_op jit(solution)/shard_map/second/pallas_call | solution.py:322
Async XLA Ops:
  1.5 19.0 %collective-permute-start = (bf16[2,64,2048]{2,1,0:T(8,128)(2,1)}, bf16[2,64,2048]{2,1,0:T(8,128)(2,1)S(1)}, u32[]{:S(2)}, u32[]{:S(2)}) collective-permute-start(bf16[2,64,2048]{2,1,0:T(8,128)(2,1)} %get-tuple-element.8), channel_id=1, source_target_pairs={{0,64},{64,0},{1,65},{65,1},{2,66},{66,2},{3,67},{67,3},{4,68},{68... | collective-permute-start | bytes 1572872 | tf_op jit(solution)/shard_map/ppermute | solution.py:355
  20.5 0.8 copy-start

commit v4 on v3

--- a/solution.py
+++ b/solution.py
@@ -28,7 +28,7 @@
     first = first.reshape(2, n // CLASSES, CLASSES, 2 * depth).transpose(2, 0, 1, 3)
     both = np.stack([cos[:, : n // 2], -sin[:, : n // 2]]) * (1.0 / n)
     both = both.reshape(2, parts, slab // 2, 2, n // 2).transpose(3, 1, 0, 2, 4)
-    second = both.reshape(2, n, n // 2)
+    second = both.reshape(2, n, -1, TILE).transpose(2, 0, 1, 3)
     order = np.zeros((2, 2, slab, 2, 2, 2, slab // 2))
     for m in range(2):
         for r in range(2):
@@ -38,7 +38,7 @@
     return first.astype(BF16), second.astype(BF16), order.astype(BF16)
 
 
-def wave_kernel(direct, flag, wind, enter, noise, keep, filt, table, *rest):
+def wave_kernel(turn, core, row, wind, enter, noise, keep, filt, table, *rest):
     (
         part, last, enter_v, noise_v, keep_v, filt_v, table_v, part_v, last_v,
         ea, cb, sb, state, z, zz, sems,
@@ -47,22 +47,21 @@
     parts, frames = part.shape[1], part.shape[3]
     depth = n // FOLD
     blocks = steps // SPAN
-    entry = enter if direct else enter_v
 
     def noise_copy(i):
         at = pl.ds(i * SPAN, SPAN)
-        return pltpu.make_async_copy(noise.at[:, at], noise_v.at[:, at], sems.at[4 + i])
+        return pltpu.make_async_copy(noise.at[:, at], noise_v.at[:, at], sems.at[5 + i])
 
     def part_copy(q):
-        return pltpu.make_async_copy(part_v.at[q], part.at[:, :, q], sems.at[4 + blocks + q])
+        return pltpu.make_async_copy(part_v.at[q], part.at[:, :, q], sems.at[5 + blocks + q])
 
     def scan(i, rb):
         rows = pl.ds(pl.multiple_of(rb * ROWS, ROWS), ROWS)
         for j in range(depth // 128):
             at = [slice(j * 128 + h * depth, j * 128 + h * depth + 128) for h in range(FOLD)]
             if i == 0:
-                re = [entry[0, rows, c].astype(F32) for c in at]
-                im = [entry[1, rows, c].astype(F32) for c in at]
+                re = [enter_v[0, rows, c].astype(F32) for c in at]
+                im = [enter_v[1, rows, c].astype(F32) for c in at]
             else:
                 re = [state[0, rows, c] for c in at]
                 im = [state[1, rows, c] for c in at]
@@ -108,7 +107,7 @@
         def waves(k):
             return jnp.where(k >= n // 2, k - n, k).astype(F32) * angle
 
-        pa = waves(line + flag[1]) * across
+        pa = waves(line + row[0]) * across
         fine = lane[:steps].astype(F32) * angle * down
         coarse = waves(lane[:steps] * 128) * down
         ca, sa = jnp.cos(pa), jnp.sin(pa)
@@ -158,15 +157,14 @@
                     both.append(pair.reshape(parts, piece, 2 * slab))
                 part_v[q, o, :, f] = jnp.concatenate(both, axis=1).astype(BF16)
 
-    @pl.when(flag[0] == 1)
+    @pl.when(core[0] == turn)
     def _():
         heads = [
-            pltpu.make_async_copy(keep, keep_v, sems.at[1]),
-            pltpu.make_async_copy(filt, filt_v, sems.at[2]),
+            pltpu.make_async_copy(keep, keep_v, sems.at[2]),
+            pltpu.make_async_copy(filt, filt_v, sems.at[3]),
+            pltpu.make_async_copy(enter, enter_v, sems.at[4]),
         ]
-        if not direct:
-            heads.append(pltpu.make_async_copy(enter, enter_v, sems.at[0]))
-        full = pltpu.make_async_copy(table, table_v, sems.at[3])
+        full = pltpu.make_async_copy(table, table_v, sems.at[1])
         for c in heads:
             c.start()
         noise_copy(0).start()
@@ -198,24 +196,21 @@
             part_copy(q).wait()
 
 
-def wave_call(flag, wind, enter, noise, keep, filt, table, parts, part=None):
+def wave_call(turn, core, row, wind, enter, noise, keep, filt, table, parts, part=None):
     steps, slab, n = noise.shape[1:]
-    direct = part is not None
     anywhere = pl.BlockSpec(memory_space=pl.ANY)
-    inside = pl.BlockSpec(memory_space=pltpu.VMEM)
-    scalars = pl.BlockSpec(memory_space=pltpu.SMEM)
-    in_specs = [scalars, scalars, inside if direct else anywhere] + [anywhere] * 4
-    args = [flag, wind, enter, noise, keep, filt, table]
+    in_specs = [pl.BlockSpec(memory_space=pltpu.SMEM)] * 3 + [anywhere] * 5
+    args = [core, row, wind, enter, noise, keep, filt, table]
     alias = {}
-    if direct:
+    if part is not None:
         in_specs.append(anywhere)
         args.append(part)
-        alias = {7: 0}
+        alias = {8: 0}
     blocks = steps // SPAN
     piece = slab // FOLD
     depth = n // FOLD
     return pl.pallas_call(
-        functools.partial(wave_kernel, direct),
+        functools.partial(wave_kernel, turn),
         out_shape=(
             jax.ShapeDtypeStruct((2, parts, FOLD, steps // 2, piece, 2 * slab), BF16),
             jax.ShapeDtypeStruct((2, slab, n), BF16),
@@ -223,7 +218,7 @@
         in_specs=in_specs,
         out_specs=[anywhere, anywhere],
         scratch_shapes=[
-            pltpu.VMEM((2, 8, 128) if direct else enter.shape, enter.dtype),
+            pltpu.VMEM(enter.shape, enter.dtype),
             pltpu.VMEM(noise.shape, noise.dtype),
             pltpu.VMEM(keep.shape, F32),
             pltpu.VMEM(filt.shape, F32),
@@ -236,7 +231,7 @@
             pltpu.VMEM((2, slab, n), F32),
             pltpu.VMEM((FOLD, steps, slab, 2 * depth), BF16),
             pltpu.VMEM((2, steps * slab, depth), BF16),
-            pltpu.SemaphoreType.DMA((4 + blocks + FOLD,)),
+            pltpu.SemaphoreType.DMA((5 + blocks + FOLD,)),
         ],
         input_output_aliases=alias,
         compiler_params=pltpu.CompilerParams(vmem_limit_bytes=VMEM),
@@ -244,44 +239,46 @@
     )(*args)
 
 
-TILE = 512
-GATHER = 2
-
-
-def second_kernel(start, table, order, got, *rest):
-    out, left, done, sems = rest[-4:]
+TILE = 256
+GATHER = 4
+
+
+def second_kernel(table, order, got, out, got_v, left, done, sems):
     parts, _, frames, piece, lanes = got.shape[1:]
     slab = FOLD * piece
-    tile = table.shape[2]
     half = out.shape[2] // 2
-    step = pl.program_id(0)
-
-    @pl.when(step < GATHER)
-    def _():
-        for m in range(0, parts, 2):
-            two = [(got[0, m + k] + got[1, m + k]).reshape(frames * slab, lanes) for k in range(2)]
+    tiles = half // TILE
+    some = parts // GATHER
+
+    def take(g):
+        at = pl.ds(g * some, some)
+        return pltpu.make_async_copy(got.at[:, at], got_v.at[:, at], sems.at[g])
+
+    def give(i, h, w):
+        lo = i * TILE + h * half + w * lanes
+        return pltpu.make_async_copy(
+            done.at[h, i, w], out.at[:, :, pl.ds(lo, lanes)], sems.at[GATHER + tiles + (h * tiles + i) * (TILE // lanes) + w]
+        )
+
+    for g in range(GATHER):
+        take(g).start()
+    for g in range(GATHER):
+        take(g).wait()
+        for m in range(g * some, (g + 1) * some, 2):
+            two = [
+                (got_v[0, m + k] + got_v[1, m + k]).reshape(frames * slab, lanes)
+                for k in range(2)
+            ]
             both = jnp.dot(
                 jnp.concatenate(two, axis=1), order[...], preferred_element_type=F32
-            )
-            at = pl.multiple_of((step * parts + m) * slab, lanes)
+            ).astype(BF16)
             for p in range(2):
-                left[p, :, pl.ds(at, lanes)] = both[:, p * lanes : (p + 1) * lanes].astype(BF16)
-
-    def copy(i, h, w):
-        lo = pl.multiple_of(i * tile + h * half + w * lanes, lanes)
-        return pltpu.make_async_copy(
-            done.at[h, i, w], out.at[pl.ds(start, frames), :, pl.ds(lo, lanes)], sems.at[h, i, w]
-        )
-
-    tiles = half // tile
-
-    @pl.when(step >= GATHER)
-    def _():
-        i = step - GATHER
-        even = jnp.dot(left[0], table[0], preferred_element_type=F32)
-        odd = jnp.dot(left[1], table[1], preferred_element_type=F32)
+                left[p, :, m * slab : (m + 2) * slab] = both[:, p * lanes : (p + 1) * lanes]
+    for i in range(tiles):
+        even = jnp.dot(left[0], table[i, 0], preferred_element_type=F32)
+        odd = jnp.dot(left[1], table[i, 1], preferred_element_type=F32)
         for h, both in enumerate((even + odd, even - odd)):
-            for w in range(tile // lanes):
+            for w in range(TILE // lanes):
                 for q in range(FOLD):
                     for f in range(frames):
                         for p in range(2):
@@ -290,53 +287,34 @@
                             done[h, i, w, f, at, :] = both[
                                 a : a + piece // 2, w * lanes : (w + 1) * lanes
                             ]
-                copy(i, h, w).start()
-
-    @pl.when(step == GATHER + tiles - 1)
-    def _():
-        for i in range(tiles):
-            for h in range(2):
-                for w in range(tile // lanes):
-                    copy(i, h, w).wait()
-
-
-def second_call(table, order, got, start, total, out=None):
+                give(i, h, w).start()
+    for i in range(tiles):
+        for h in range(2):
+            for w in range(TILE // lanes):
+                give(i, h, w).wait()
+
+
+def second_call(table, order, got):
     parts, _, frames, piece, lanes = got.shape[1:]
     slab = FOLD * piece
-    depth, half = table.shape[1:]
-    tile = TILE
-    in_specs = [
-        pl.BlockSpec((2, depth, tile), lambda i: (0, 0, jnp.maximum(i - GATHER, 0))),
-        pl.BlockSpec(order.shape, lambda i: (0, 0)),
-        pl.BlockSpec(
-            (2, parts // GATHER, FOLD, frames, piece, lanes),
-            lambda i: (0, jnp.minimum(i, GATHER - 1), 0, 0, 0, 0),
-        ),
-    ]
-    args = [table, order, got]
-    alias = {}
-    if out is not None:
-        in_specs.append(pl.BlockSpec(memory_space=pl.ANY))
-        args.append(out)
-        alias = {3: 0}
+    tiles, _, depth, _ = table.shape
+    half = tiles * TILE
+    anywhere = pl.BlockSpec(memory_space=pl.ANY)
+    inside = pl.BlockSpec(memory_space=pltpu.VMEM)
     return pl.pallas_call(
-        functools.partial(second_kernel, start),
-        out_shape=jax.ShapeDtypeStruct((total, slab, 2 * half), F32),
-        grid=(GATHER + half // tile,),
-        in_specs=in_specs,
-        out_specs=pl.BlockSpec(memory_space=pl.ANY),
+        second_kernel,
+        out_shape=jax.ShapeDtypeStruct((frames, slab, 2 * half), F32),
+        in_specs=[inside, inside, anywhere],
+        out_specs=anywhere,
         scratch_shapes=[
+            pltpu.VMEM(got.shape, BF16),
             pltpu.VMEM((2, frames * slab, depth), BF16),
-            pltpu.VMEM((2, half // tile, tile // lanes, frames, slab, lanes), F32),
-            pltpu.SemaphoreType.DMA((2, half // tile, tile // lanes)),
+            pltpu.VMEM((2, tiles, TILE // lanes, frames, slab, lanes), F32),
+            pltpu.SemaphoreType.DMA((GATHER + tiles + 2 * half // lanes,)),
         ],
-        input_output_aliases=alias,
-        compiler_params=pltpu.CompilerParams(vmem_limit_bytes=VMEM),
-        cost_estimate=pl.CostEstimate(
-            flops=4 * depth * half * frames * slab, bytes_accessed=20 << 20, transcendentals=0
-        ),
+        compiler_params=pltpu.CompilerParams(vmem_limit_bytes=26 * 1024 * 1024),
         name="second",
-    )(*args)
+    )(table, order, got)
 
 
 def shards(innovation, retention, rytov_filter, wind_shift, start_state):
@@ -347,17 +325,16 @@
     parts = lax.axis_size("mode")
     first, second, order = tables(n, parts)
 
-    core = lax.axis_index("tm").astype(jnp.int32)
-    row = lax.axis_index("mode").astype(jnp.int32) * slab
     start = start_state.reshape(2, slab, n)
-    flags = [jnp.stack([on, row]) for on in (1 - core, core)]
-    part, last = wave_call(flags[0], wind, start, noise, keep, filt, first, parts)
+    core = lax.axis_index("tm").astype(jnp.int32)[None]
+    row = (lax.axis_index("mode").astype(jnp.int32) * slab)[None]
+    part, last = wave_call(0, core, row, wind, start, noise, keep, filt, first, parts)
     enter = lax.ppermute(last, "tm", [(0, 1), (1, 0)])
-    part, _ = wave_call(flags[1], wind, enter, noise, keep, filt, first, parts, part)
+    part, _ = wave_call(1, core, row, wind, enter, noise, keep, filt, first, parts, part)
     got = lax.all_to_all(
         part.reshape((2 * parts,) + part.shape[2:]), ("layer", "mode"), 0, 0, tiled=True
     ).reshape(part.shape)
-    return second_call(second, order, got, 0, steps // 2)
+    return second_call(second, order, got)
 
 
 def solution(mesh):

time: 145 us -> 141 us (0.972)
  Pallas kernels: 29.9 us -> 25.8 us
    pallas_call x3, Pallas kernels: 29.9 us -> 25.8 us  [the longest x2 17.5 us: wave_call(): pl.pallas_call(functools.partial(wave_kernel, turn), out_shape=(jax.Shape...]
where the time goes in v4:
time: 141 us; the launch traced here: 140 us
  blocking collectives  94 us (67%)
  Pallas kernels  25.8 us (18%)
  starting transfers between devices  17.3 us (12%)
  waiting for transfers between devices  1.75 us (1%)
    all_to_all x1, blocking collectives, shards(): lax.all_to_all(part.reshape((2 * parts,) + part.shape[2:]), ('layer', 'mo...  94 us
    pallas_call x2, Pallas kernels, wave_call(): pl.pallas_call(functools.partial(wave_kernel, turn), out_shape=(jax.Shape...  17.5 us
    ppermute x1, starting transfers between devices, shards(): enter = lax.ppermute(last, 'tm', [(0, 1), (1, 0)])  17.3 us
    pallas_call x1, Pallas kernels, second_call(): pl.pallas_call(second_kernel, out_shape=jax.ShapeDtypeStruct((frames, sla...  8.34 us
  transfers between devices with their start and end apart: 1, of which 1 were waited for; matrix products, arithmetic and copies ran while one was open for 0% of the time, Pallas kernels for 0%

profile of v4, /device:TPU:1, one launch (start us, length us, event | category | flops | bytes accessed | tf_op | source)
XLA Modules:
  0.0 139.9 jit_solution(2915159491716932765)
XLA Ops:
  0.0 0.8 wave.2
  0.8 17.3 %collective-permute-start = (bf16[2,64,2048]{2,1,0:T(8,128)(2,1)}, bf16[2,64,2048]{2,1,0:T(8,128)(2,1)S(1)}, u32[]{:S(2)}, u32[]{:S(2)}) collective-permute-start(bf16[2,64,2048]{2,1,0:T(8,128)(2,1)} %get-tuple-element.8), channel_id=1, source_target_pairs={{0,64},{64,0},{1,65},{65,1},{2,66},{66,2},{3,67},{67,3},{4,68},{68... | collective-permute-start | bytes 1572872 | tf_op jit(solution)/shard_map/ppermute | solution.py:332
  18.1 1.7 %collective-permute-done.enter = bf16[2,64,2048]{2,1,0:T(8,128)(2,1)S(1)} collective-permute-done((bf16[2,64,2048]{2,1,0:T(8,128)(2,1)}, bf16[2,64,2048]{2,1,0:T(8,128)(2,1)S(1)}, u32[]{:S(2)}, u32[]{:S(2)}) %collective-permute-start) | collective-permute-done | bytes 524320 | tf_op jit(solution)/shard_map/ppermute | solution.py:332
  19.9 0.0 copy-start.2
  19.9 0.8 copy-done.2
  20.7 16.6 %wave.3 = (bf16[2,32,4,8,16,128]{5,4,3,2,1,0:T(8,128)(2,1)}, bf16[2,64,2048]{2,1,0:T(8,128)(2,1)}) custom-call(s32[1]{0:T(128)} %bitcast.core, s32[1]{0:T(128)} %bitcast.1.row, f32[2,16]{1,0:T(2,128)} %bitcast.21, bf16[2,64,2048]{2,1,0:T(8,128)(2,1)} %copy-done.2, bf16[2,16,64,2048]{3,2,1,0:T(8,128)(2,1)} %bitcast.13, ...), custom_call_target="tpu_custom_call", output_to_operand_aliasing={{0}: (8, {})} | custom-call | tf_op jit(solution)/shard_map/wave/pallas_call | solution.py:212
  37.3 0.0 copy-start
  37.3 0.0 copy-start.1
  37.4 94.0 %all_to_all.5 = bf16[64,4,8,16,128]{4,3,2,1,0:T(8,128)(2,1)S(1)} all-to-all(bf16[64,4,8,16,128]{4,3,2,1,0:T(8,128)(2,1)} %bitcast.14), channel_id=1, replica_groups=mesh['tm'=2,'layer'=2,'mode'=32] {'layer','mode'}, dimensions={0} | all-to-all | bytes 16777216 | tf_op jit(solution)/shard_map/all_to_all | solution.py:334
  131.3 0.0 copy-done
  131.3 0.0 copy-done.1
  131.3 8.3 %second.1 = f32[8,64,2048]{2,1,0:T(8,128)} custom-call(bf16[4,2,2048,256]{3,2,1,0:T(8,128)(2,1)S(1)} %copy-done, bf16[256,256]{1,0:T(8,128)(2,1)S(1)} %copy-done.1, bf16[2,32,4,8,16,128]{5,4,3,2,1,0:T(8,128)(2,1)S(1)} %bitcast.11), custom_call_target="tpu_custom_call" | custom-call | tf_op jit(solution)/shard_map/second/pallas_call | solution.py:304
Async XLA Ops:
  0.8 19.1 %collective-permute-start = (bf16[2,64,2048]{2,1,0:T(8,128)(2,1)}, bf16[2,64,2048]{2,1,0:T(8,128)(2,1)S(1)}, u32[]{:S(2)}, u32[]{:S(2)}) collective-permute-start(bf16[2,64,2048]{2,1,0:T(8,128)(2,1)} %get-tuple-element.8), channel_id=1, source_target_pairs={{0,64},{64,0},{1,65},{65,1},{2,66},{66,2},{3,67},{67,3},{4,68},{68... | collective-permute-start | bytes 1572872 | tf_op jit(solution)/shard_map/ppermute | solution.py:332
  19.9 0.8 copy-start.2
  37.3 94.0 %copy-start = (bf16[4,2,2048,256]{3,2,1,0:T(8,128)(2,1)S(1)}, bf16[4,2,2048,256]{3,2,1,0:T(8,128)(2,1)}, u32[]{:S(2)}) copy-start(bf16[4,2,2048,256]{3,2,1,0:T(8,128)(2,1)} %constant.19.clone.table) | copy-start | bytes 25165828
  37.3 94.0 %copy-start.1 = (bf16[256,256]{1,0:T(8,128)(2,1)S(1)}, bf16[256,256]{1,0:T(8,128)(2,1)}, u32[]{:S(2)}) copy-start(bf16[256,256]{1,0:T(8,128)(2,1)} %constant.20.clone.order) | copy-start | bytes 393220

commit v5 on v4

--- a/solution.py
+++ b/solution.py
@@ -169,9 +169,9 @@
             c.start()
         noise_copy(0).start()
         noise_copy(1).start()
-        full.start()
         for i in range(2, blocks):
             noise_copy(i).start()
+        full.start()
         turns()
         for c in heads:
             c.wait()
@@ -240,7 +240,7 @@
 
 
 TILE = 256
-GATHER = 4
+GATHER = 2
 
 
 def second_kernel(table, order, got, out, got_v, left, done, sems):

time: 141 us -> 141 us (level)
  no operation moved by 1% of the time
where the time goes in v5:
time: 141 us; the launch traced here: 140 us
  blocking collectives  94 us (67%)
  Pallas kernels  25.5 us (18%)
  starting transfers between devices  17.3 us (12%)
  waiting for transfers between devices  1.75 us (1%)
    all_to_all x1, blocking collectives, shards(): lax.all_to_all(part.reshape((2 * parts,) + part.shape[2:]), ('layer', 'mo...  94 us
    pallas_call x2, Pallas kernels, wave_call(): pl.pallas_call(functools.partial(wave_kernel, turn), out_shape=(jax.Shape...  17.5 us
    ppermute x1, starting transfers between devices, shards(): enter = lax.ppermute(last, 'tm', [(0, 1), (1, 0)])  17.3 us
    pallas_call x1, Pallas kernels, second_call(): pl.pallas_call(second_kernel, out_shape=jax.ShapeDtypeStruct((frames, sla...  8.05 us
  transfers between devices with their start and end apart: 1, of which 1 were waited for; matrix products, arithmetic and copies ran while one was open for 0% of the time, Pallas kernels for 0%

profile of v5, /device:TPU:1, one launch (start us, length us, event | category | flops | bytes accessed | tf_op | source)
XLA Modules:
  0.0 139.6 jit_solution(4254611772718673986)
XLA Ops:
  0.0 0.8 wave.2
  0.8 17.3 %collective-permute-start = (bf16[2,64,2048]{2,1,0:T(8,128)(2,1)}, bf16[2,64,2048]{2,1,0:T(8,128)(2,1)S(1)}, u32[]{:S(2)}, u32[]{:S(2)}) collective-permute-start(bf16[2,64,2048]{2,1,0:T(8,128)(2,1)} %get-tuple-element.8), channel_id=1, source_target_pairs={{0,64},{64,0},{1,65},{65,1},{2,66},{66,2},{3,67},{67,3},{4,68},{68... | collective-permute-start | bytes 1572872 | tf_op jit(solution)/shard_map/ppermute | solution.py:332
  18.1 1.7 %collective-permute-done.enter = bf16[2,64,2048]{2,1,0:T(8,128)(2,1)S(1)} collective-permute-done((bf16[2,64,2048]{2,1,0:T(8,128)(2,1)}, bf16[2,64,2048]{2,1,0:T(8,128)(2,1)S(1)}, u32[]{:S(2)}, u32[]{:S(2)}) %collective-permute-start) | collective-permute-done | bytes 524320 | tf_op jit(solution)/shard_map/ppermute | solution.py:332
  19.9 0.0 copy-start.2
  19.9 0.8 copy-done.2
  20.7 16.6 %wave.3 = (bf16[2,32,4,8,16,128]{5,4,3,2,1,0:T(8,128)(2,1)}, bf16[2,64,2048]{2,1,0:T(8,128)(2,1)}) custom-call(s32[1]{0:T(128)} %bitcast.core, s32[1]{0:T(128)} %bitcast.1.row, f32[2,16]{1,0:T(2,128)} %bitcast.21, bf16[2,64,2048]{2,1,0:T(8,128)(2,1)} %copy-done.2, bf16[2,16,64,2048]{3,2,1,0:T(8,128)(2,1)} %bitcast.13, ...), custom_call_target="tpu_custom_call", output_to_operand_aliasing={{0}: (8, {})} | custom-call | tf_op jit(solution)/shard_map/wave/pallas_call | solution.py:212
  37.3 0.0 copy-start
  37.3 0.0 copy-start.1
  37.4 94.0 %all_to_all.5 = bf16[64,4,8,16,128]{4,3,2,1,0:T(8,128)(2,1)S(1)} all-to-all(bf16[64,4,8,16,128]{4,3,2,1,0:T(8,128)(2,1)} %bitcast.14), channel_id=1, replica_groups=mesh['tm'=2,'layer'=2,'mode'=32] {'layer','mode'}, dimensions={0} | all-to-all | bytes 16777216 | tf_op jit(solution)/shard_map/all_to_all | solution.py:334
  131.3 0.0 copy-done
  131.3 0.0 copy-done.1
  131.3 8.0 %second.1 = f32[8,64,2048]{2,1,0:T(8,128)} custom-call(bf16[4,2,2048,256]{3,2,1,0:T(8,128)(2,1)S(1)} %copy-done, bf16[256,256]{1,0:T(8,128)(2,1)S(1)} %copy-done.1, bf16[2,32,4,8,16,128]{5,4,3,2,1,0:T(8,128)(2,1)S(1)} %bitcast.11), custom_call_target="tpu_custom_call" | custom-call | tf_op jit(solution)/shard_map/second/pallas_call | solution.py:304
Async XLA Ops:
  0.8 19.1 %collective-permute-start = (bf16[2,64,2048]{2,1,0:T(8,128)(2,1)}, bf16[2,64,2048]{2,1,0:T(8,128)(2,1)S(1)}, u32[]{:S(2)}, u32[]{:S(2)}) collective-permute-start(bf16[2,64,2048]{2,1,0:T(8,128)(2,1)} %get-tuple-element.8), channel_id=1, source_target_pairs={{0,64},{64,0},{1,65},{65,1},{2,66},{66,2},{3,67},{67,3},{4,68},{68... | collective-permute-start | bytes 1572872 | tf_op jit(solution)/shard_map/ppermute | solution.py:332
  19.9 0.8 copy-start.2
  37.3 94.0 %copy-start = (bf16[4,2,2048,256]{3,2,1,0:T(8,128)(2,1)S(1)}, bf16[4,2,2048,256]{3,2,1,0:T(8,128)(2,1)}, u32[]{:S(2)}) copy-start(bf16[4,2,2048,256]{3,2,1,0:T(8,128)(2,1)} %constant.19.clone.table) | copy-start | bytes 25165828
  37.3 94.0 %copy-start.1 = (bf16[256,256]{1,0:T(8,128)(2,1)S(1)}, bf16[256,256]{1,0:T(8,128)(2,1)}, u32[]{:S(2)}) copy-start(bf16[256,256]{1,0:T(8,128)(2,1)} %constant.20.clone.order) | copy-start | bytes 393220
